TPU v7x, 768 devices: a whole 4x8x12 slice. The times are simulated.
768 devices in a mesh: dp: 96 (over y, x, z_hi), head: 8 (over z_lo, core).
Axes of the slice: x: 4, y: 8, z: 12 (z_hi: 3, z_lo: 4; z = z_hi * 4 + z_lo), core: 2. Of those that a mesh axis runs over, the one named last changes fastest.
Arguments:
- tokens: bfloat16 [24576, 2048], P('dp'), may hold values from -6 to 6
- weights: bfloat16 [8, 768, 2048], P('head', 'dp'), may hold values from -0.13479223 to 0.13479223, as said below
- query_gain: float32 [128], replicated, may hold values from 0.25 to 1.75
- key_gain: float32 [128], replicated, may hold values from 0.25 to 1.75
- first_row: int32 [24576], P('dp'), may hold values from 0 to 24575, as said below
- cotangent: bfloat16 [24576, 4096], P('dp', 'head'), may hold values from -6 to 6
Outputs:
- attended: bfloat16 [24576, 4096], P('dp', 'head')
- token_grad: bfloat16 [24576, 2048], P('dp', 'head')
- weight_grad: float32 [8, 768, 2048], P('head', 'dp')
Inputs may be any that keep to these rules, and one draw needn't show every extreme that they name: first_row[i] is the position of the first row of row i's document: documents are runs of consecutive rows, each at most 512 rows long, one of exactly 512 rows, and the last row begins a document of its own. For every even g, weights[g] and weights[g + 1] are equal in their last 256 rows: each key-value head is held by two head devices.
All inputs are finite; a program needn't handle non-finite values.
Results may differ from a plain program's by a relative error of at most 0.017.
Values may be sent and summed in bfloat16 or wider, within the bound.
A program may use at most 32 MiB of HBM per device.

v0:
```python
import math

import jax
import jax.numpy as jnp
from jax import lax
from jax.sharding import PartitionSpec as P

HD = 128
QH_DEV = 4
COLS = 768
ROWS = 256
SPAN = 2


EPSILON = 1e-06
THETA = 1000000.0
STRETCH = 0.25


def from_behind(x, axis, by):
    devices = lax.axis_size(axis)
    pairs = [(i, i + by) for i in range(devices) if 0 <= i + by < devices]
    return lax.ppermute(x, axis, pairs)


def partner(x, axis, apart):
    return lax.ppermute(x, axis, [(i, i ^ 1 << apart) for i in range(lax.axis_size(axis))])


def rope_tables(position, head_size):
    middle = head_size // 2
    channel = jnp.arange(middle, dtype=jnp.float32)
    frequency = THETA ** (-2.0 * channel / head_size)
    angles = (position.astype(jnp.float32) * STRETCH)[:, None] * frequency[None, :]
    angles = jnp.concatenate([angles, angles], axis=1)
    return (jnp.cos(angles), jnp.sin(angles))


def normalize_rotate(values, scaling, cosine_table, sine_table):
    factor = lax.rsqrt(jnp.mean(values * values, axis=-1, keepdims=True) + EPSILON)
    normed = values * factor * scaling
    middle = normed.shape[-1] // 2
    turned = jnp.concatenate([-normed[..., middle:], normed[..., :middle]], axis=-1)
    return normed * cosine_table + turned * sine_table


def prepare(projected, query_gain, key_gain, cosine_table, sine_table):
    row_count = projected.shape[0]
    queries = projected[:, : QH_DEV * HD].reshape(row_count, QH_DEV, HD)
    queries = normalize_rotate(
        queries, query_gain, cosine_table[:, None, :], sine_table[:, None, :]
    )
    key_part = normalize_rotate(
        projected[:, QH_DEV * HD : (QH_DEV + 1) * HD], key_gain, cosine_table, sine_table
    )
    value_part = projected[:, (QH_DEV + 1) * HD :]
    return (queries, key_part, value_part)


def attend_window(queries, window, upstream, first_rows, query_place, key_place):
    score_scale = 1.0 / math.sqrt(HD)
    key_window = window[:, :HD]
    value_window = window[:, HD:]
    visible = (key_place[None, :] >= first_rows[:, None]) & (
        key_place[None, :] <= query_place[:, None]
    )
    score = (
        jnp.einsum("rhc,kc->rhk", queries, key_window, preferred_element_type=jnp.float32)
        * score_scale
    )
    weight = jnp.where(visible[:, None, :], jnp.exp(score), 0.0)
    denominator = jnp.sum(weight, axis=-1)
    summed = jnp.einsum(
        "rhk,kc->rhc", weight.astype(jnp.bfloat16), value_window, preferred_element_type=jnp.float32
    )
    attended = (summed / denominator[..., None]).astype(jnp.bfloat16)
    probability = weight / denominator[..., None]
    row_delta = jnp.sum(upstream.astype(jnp.float32) * attended.astype(jnp.float32), axis=-1)
    grad_prob = jnp.einsum(
        "rhc,kc->rhk", upstream, value_window, preferred_element_type=jnp.float32
    )
    grad_score = (probability * (grad_prob - row_delta[..., None]) * score_scale).astype(
        jnp.bfloat16
    )
    grad_query = jnp.einsum(
        "rhk,kc->rhc", grad_score, key_window, preferred_element_type=jnp.float32
    )
    grad_key = jnp.einsum("rhk,rhc->kc", grad_score, queries, preferred_element_type=jnp.float32)
    grad_value = jnp.einsum(
        "rhk,rhc->kc",
        probability.astype(jnp.bfloat16),
        upstream,
        preferred_element_type=jnp.float32,
    )
    return (attended, grad_query, jnp.concatenate([grad_key, grad_value], axis=1))


def body(tokens, weights, query_gain, key_gain, first_row, cotangent):
    block_index = lax.axis_index("dp")
    position = block_index * ROWS + jnp.arange(ROWS, dtype=jnp.int32)
    key_place = (block_index - SPAN) * ROWS + jnp.arange((SPAN + 1) * ROWS, dtype=jnp.int32)
    cosine_table, sine_table = rope_tables(position, HD)
    weight_piece = lax.all_gather(weights, "dp", axis=1, tiled=True)
    projected = jnp.einsum("rd,cd->rc", tokens, weight_piece[0], preferred_element_type=jnp.float32)
    prepared, pullback = jax.vjp(
        lambda values: prepare(values, query_gain, key_gain, cosine_table, sine_table), projected
    )
    queries = prepared[0].astype(jnp.bfloat16)
    key_value = jnp.concatenate([prepared[1], prepared[2]], axis=1).astype(jnp.bfloat16)
    earlier = [from_behind(key_value, "dp", distance) for distance in range(SPAN, 0, -1)]
    window = jnp.concatenate(earlier + [key_value], axis=0)
    upstream = cotangent.reshape(ROWS, QH_DEV, HD)
    attended, grad_query, slot_grads = attend_window(
        queries, window, upstream, first_row, position, key_place
    )
    pair_grad = slot_grads[SPAN * ROWS :]
    for distance in range(1, SPAN + 1):
        slot_index = SPAN - distance
        pair_grad = pair_grad + from_behind(
            slot_grads[slot_index * ROWS : (slot_index + 1) * ROWS].astype(jnp.bfloat16),
            "dp",
            -distance,
        ).astype(jnp.float32)
    grad_projected = pullback((grad_query, pair_grad[:, :HD], pair_grad[:, HD:]))[0].astype(
        jnp.bfloat16
    )
    partial_grad = jnp.dot(grad_projected, weight_piece[0], preferred_element_type=jnp.float32)
    token_grad = lax.psum_scatter(
        partial_grad.astype(jnp.bfloat16), "head", scatter_dimension=1, tiled=True
    )
    shard_rows = COLS // lax.axis_size("dp")
    own_grad = lax.psum_scatter(
        jnp.einsum("rc,rd->cd", grad_projected, tokens, preferred_element_type=jnp.float32),
        "dp",
        scatter_dimension=0,
        tiled=True,
    )
    partner_grad = partner(own_grad.astype(jnp.bfloat16), "head", 0).astype(own_grad.dtype)
    global_rows = block_index * shard_rows + jnp.arange(shard_rows, dtype=jnp.int32)
    shared_rows = global_rows >= QH_DEV * HD
    weight_grad = jnp.where(shared_rows[:, None], own_grad + partner_grad, own_grad)
    return (attended.reshape(ROWS, QH_DEV * HD), token_grad, weight_grad[None])


def solution(mesh):
    in_specs = (P("dp", None), P("head", "dp", None), P(), P(), P("dp"), P("dp", "head"))
    out_specs = (P("dp", "head"), P("dp", "head"), P("head", "dp", None))
    return jax.shard_map(body, mesh=mesh, in_specs=in_specs, out_specs=out_specs, check_vma=False)
```

profile of v0, /device:TPU:1, one launch (start us, length us, event | category | flops | bytes accessed | tf_op | source)
XLA Modules:
  0.0 970.4 jit_solution(9213941942881461274)
XLA Ops:
  8.0 1.8 copy.66
  9.9 1.6 compare_and_fusion
  11.5 172.8 %all-gather.2.cloned.1.call-done = bf16[1,768,2048]{2,1,0:T(8,128)(2,1)} async-done(((bf16[1,8,2048]{2,1,0:T(8,128)(2,1)}), bf16[1,768,2048]{2,1,0:T(8,128)(2,1)}) %all-gather.2.cloned.1.call-update) | async-done | bytes 3145744 | tf_op jit(solution)/shard_map/all_gather | solution.py:103
  184.3 2.9 fusion.4
  187.6 1.3 fusion.38
  189.5 10.2 %collective-permute-start.1 = (bf16[256,256]{1,0:T(8,128)(2,1)}, bf16[256,256]{1,0:T(8,128)(2,1)}, u32[]{:S(2)}, u32[]{:S(2)}) collective-permute-start(bf16[256,256]{1,0:T(8,128)(2,1)} %pad_maximum_fusion.2), channel_id=1, source_target_pairs={{0,8},{8,16},{16,24},{24,32},{32,40},{40,48},{48,56},{56,64},{64,7... | collective-permute-start | bytes 393224 | tf_op jit(solution)/shard_map/ppermute | solution.py:23
  199.7 1.9 collective-permute-start
  202.5 1.0 copy.63
  204.0 1.0 maximum_maximum_fusion
  205.1 1.0 fusion.10
  206.1 1.4 multiply_reduce_fusion.1
  207.6 1.1 fusion.19
  208.6 1.5 fusion.1
  212.4 1.3 collective-permute-start.2
  213.7 1.3 collective-permute-start.3
  215.4 12.0 %collective-permute-done.2 = bf16[256,256]{1,0:T(8,128)(2,1)} collective-permute-done((bf16[256,256]{1,0:T(8,128)(2,1)}, bf16[256,256]{1,0:T(8,128)(2,1)}, u32[]{:S(2)}, u32[]{:S(2)}) %collective-permute-start.2) | collective-permute-done | bytes 131104 | tf_op jit(solution)/shard_map/ppermute | solution.py:23
  227.4 3.1 collective-permute-done.3
  230.5 1.1 fusion.34
  233.0 3.7 fusion.48
  236.8 3.9 fusion.6
  240.7 612.8 %reduce-scatter.5.cloned.1.call-done = f32[8,2048]{1,0:T(8,128)} async-done(((f32[768,2048]{1,0:T(8,128)}), f32[8,2048]{1,0:T(8,128)}) %reduce-scatter.5.cloned.1.call-update) | async-done | bytes 65552 | tf_op jit(solution)/shard_map/reduce_scatter | solution.py:132
  854.3 79.2 %collective-permute-start.4 = (bf16[8,2048]{1,0:T(8,128)(2,1)S(1)}, bf16[8,2048]{1,0:T(8,128)(2,1)S(1)}, u32[]{:S(2)}, u32[]{:S(2)}) collective-permute-start(bf16[8,2048]{1,0:T(8,128)(2,1)S(1)} %convert_element_type.61), channel_id=1, source_target_pairs={{0,1},{1,0},{2,3},{3,2},{4,5},{5,4},{6,7},{7,6},{8,9},{9,8},{10,11... | collective-permute-start | bytes 98312 | tf_op jit(solution)/shard_map/ppermute | solution.py:27
  934.4 1.5 fusion.41
  935.9 27.9 %reduce-scatter.3.cloned.1.call-done = bf16[256,256]{1,0:T(8,128)(2,1)} async-done(((bf16[256,2048]{1,0:T(8,128)(2,1)}), bf16[256,256]{1,0:T(8,128)(2,1)}) %reduce-scatter.3.cloned.1.call-update) | async-done | bytes 131088 | tf_op jit(solution)/shard_map/reduce_scatter | solution.py:128
  (61 shorter events, 9.0 us)
Async XLA Ops:
  7.2 177.1 %copy-start = (bf16[256,2048]{1,0:T(8,128)(2,1)S(1)}, bf16[256,2048]{1,0:T(8,128)(2,1)}, u32[]{:S(2)}) copy-start(bf16[256,2048]{1,0:T(8,128)(2,1)} %param.6) | copy-start | bytes 3145732
  7.2 177.1 %all-gather.2.cloned.1.call-start = ((), (), s32[]{:S(2)}) async-start(), calls=%async_computation.2 | async-start | bytes 3178496 | tf_op jit(solution)/shard_map/all_gather | solution.py:103
  7.9 845.6 %reduce-scatter.5.cloned.1.call-start = ((), (), s32[]{:S(2)}) async-start(), calls=%async_computation.4 | async-start | bytes 6356992 | tf_op jit(solution)/shard_map/reduce_scatter | solution.py:132
  9.8 177.6 %copy-start.6 = (f32[128]{0:T(128)S(1)}, f32[128]{0:T(128)}, u32[]{:S(2)}) copy-start(f32[128]{0:T(128)} %param.9) | copy-start | bytes 1540
  187.3 16.4 %copy-start.5 = (f32[128]{0:T(128)S(1)}, f32[128]{0:T(128)}, u32[]{:S(2)}) copy-start(f32[128]{0:T(128)} %param.8) | copy-start | bytes 1540
  189.5 14.5 %collective-permute-start.1 = (bf16[256,256]{1,0:T(8,128)(2,1)}, bf16[256,256]{1,0:T(8,128)(2,1)}, u32[]{:S(2)}, u32[]{:S(2)}) collective-permute-start(bf16[256,256]{1,0:T(8,128)(2,1)} %pad_maximum_fusion.2), channel_id=1, source_target_pairs={{0,8},{8,16},{16,24},{24,32},{32,40},{40,48},{48,56},{56,64},{64,7... | collective-permute-start | bytes 393224 | tf_op jit(solution)/shard_map/ppermute | solution.py:23
  199.7 4.3 collective-permute-start
  203.7 1.4 copy-start.4
  203.9 2.2 copy-start.3
  208.6 3.0 copy-start.1
  212.4 15.0 %collective-permute-start.2 = (bf16[256,256]{1,0:T(8,128)(2,1)}, bf16[256,256]{1,0:T(8,128)(2,1)}, u32[]{:S(2)}, u32[]{:S(2)}) collective-permute-start(bf16[256,256]{1,0:T(8,128)(2,1)} %get-tuple-element.21), channel_id=1, source_target_pairs={{8,0},{16,8},{24,16},{32,24},{40,32},{48,40},{56,48},{64,56},{72,6... | collective-permute-start | bytes 393224 | tf_op jit(solution)/shard_map/ppermute | solution.py:23
  213.7 16.8 %collective-permute-start.3 = (bf16[256,256]{1,0:T(8,128)(2,1)}, bf16[256,256]{1,0:T(8,128)(2,1)}, u32[]{:S(2)}, u32[]{:S(2)}) collective-permute-start(bf16[256,256]{1,0:T(8,128)(2,1)} %get-tuple-element.22), channel_id=1, source_target_pairs={{16,0},{24,8},{32,16},{40,24},{48,32},{56,40},{64,48},{72,56},{80,... | collective-permute-start | bytes 393224 | tf_op jit(solution)/shard_map/ppermute | solution.py:23
  236.7 696.8 %copy-start.2 = (bf16[256,4,128]{0,2,1:T(8,128)(2,1)S(1)}, bf16[256,4,128]{0,2,1:T(8,128)(2,1)}, u32[]{:S(2)}) copy-start(bf16[256,4,128]{0,2,1:T(8,128)(2,1)} %get-tuple-element.35) | copy-start | bytes 786436
  236.7 727.1 %reduce-scatter.3.cloned.1.call-start = ((), (), s32[]{:S(2)}) async-start(), calls=%async_computation.3 | async-start | bytes 1179648 | tf_op jit(solution)/shard_map/reduce_scatter | solution.py:128
  854.3 80.1 %collective-permute-start.4 = (bf16[8,2048]{1,0:T(8,128)(2,1)S(1)}, bf16[8,2048]{1,0:T(8,128)(2,1)S(1)}, u32[]{:S(2)}, u32[]{:S(2)}) collective-permute-start(bf16[8,2048]{1,0:T(8,128)(2,1)S(1)} %convert_element_type.61), channel_id=1, source_target_pairs={{0,1},{1,0},{2,3},{3,2},{4,5},{5,4},{6,7},{7,6},{8,9},{9,8},{10,11... | collective-permute-start | bytes 98312 | tf_op jit(solution)/shard_map/ppermute | solution.py:27
Sparse Core Ops, SparseCore 0:
  13.6 170.6 all-gather.1
  236.8 616.5 reduce-scatter.4
  857.5 106.3 reduce-scatter.2
where the time goes:
time: 972 us; the launch traced here: 970 us
  waiting for transfers between devices  829 us (85%)
  starting transfers between devices  94 us (10%)
  matrix products  16.7 us (2%)
  between operations  14.1 us (1%)
  other arithmetic  10.9 us (1%)
    reduce_scatter x1, waiting for transfers between devices, body(): lax.psum_scatter(jnp.einsum('rc,rd->cd', grad_projected, tokens, preferre...  613 us
    all_gather x1, waiting for transfers between devices, body(): weight_piece = lax.all_gather(weights, 'dp', axis=1, tiled=True)  173 us
    ppermute x1, starting transfers between devices, partner(): lax.ppermute(x, axis, [(i, i ^ 1 << apart) for i in range(lax.axis_size(a...  79.2 us
    reduce_scatter x1, waiting for transfers between devices, body(): lax.psum_scatter(partial_grad.astype(jnp.bfloat16), 'head', scatter_dimen...  27.9 us
  transfers between devices with their start and end apart: 8, of which 5 were waited for; matrix products, arithmetic and copies ran while one was open for 1% of the time, Pallas kernels for 0%

commit v1 on v0

--- a/solution.py
+++ b/solution.py
@@ -3,6 +3,8 @@
 import jax
 import jax.numpy as jnp
 from jax import lax
+from jax.experimental import pallas as pl
+from jax.experimental.pallas import tpu as pltpu
 from jax.sharding import PartitionSpec as P
 
 HD = 128
@@ -17,14 +19,316 @@
 STRETCH = 0.25
 
 
+NY, NX, NZ = 8, 4, 3
+D = 2048
+CA = 896
+CB = D - CA
+CH = CB // 256 * 128
+MESH = pl.DeviceIdType.MESH
+BF, F32 = jnp.bfloat16, jnp.float32
+
+
+class Links:
+    def __init__(self, send_sem, recv_sem):
+        self.send_sem, self.recv_sem = send_sem, recv_sem
+        self.sent = []
+
+    def send(self, src, dst, target):
+        n = len(self.sent)
+        copy = pltpu.make_async_remote_copy(
+            src_ref=src, dst_ref=dst, send_sem=self.send_sem.at[n], recv_sem=self.recv_sem.at[n],
+            device_id=target, device_id_type=MESH)
+        copy.start()
+        self.sent.append(copy)
+        return copy
+
+    def finish(self):
+        for copy in self.sent:
+            copy.wait_send()
+
+
+def rounds(sequences):
+    live = list(sequences)
+    while live:
+        still = []
+        for s in live:
+            if next(s, 0) is None:
+                still.append(s)
+        live = still
+        yield
+
+
+def places():
+    dp, head = lax.axis_index("dp"), lax.axis_index("head")
+    return dp // (NX * NZ), (dp // NZ) % NX, dp % NZ, head
+
+
+def at(y, x, z, head):
+    return (((y + NY) % NY * NX + (x + NX) % NX) * NZ + (z + NZ) % NZ, head)
+
+
+def ry(y):
+    return (y + NY) % NY
+
+
+def rx(x):
+    return (x + NX) % NX
+
+
+def rz(z):
+    return (z + NZ) % NZ
+
+
+def peers(y, x, z, head):
+    out = [at(y + 1, x, z, head), at(y - 1, x, z, head)]
+    out += [at(y, x + d, z, head) for d in (1, 2, 3)]
+    out += [at(y, x, z + d, head) for d in (1, 2)]
+    return out
+
+
+def enter(targets):
+    barrier = pltpu.get_barrier_semaphore()
+    for t in targets:
+        pl.semaphore_signal(barrier, inc=1, device_id=t, device_id_type=MESH)
+    pl.semaphore_wait(barrier, len(targets))
+
+
+A = pl.ds(0, CA)
+B = pl.ds(CA, CB)
+
+
+def gather_rows(links, w, y, x, z, head):
+    up, down = at(y + 1, x, z, head), at(y - 1, x, z, head)
+    right, left, across = (at(y, x + d, z, head) for d in (1, -1, 2))
+    own = w.at[y, x, z]
+    far = [links.send(own, own, at(y, x, z + d, head)) for d in (1, 2)]
+
+    def seq_a(k):
+        r = w.at[y, x, k, :, A]
+        s = [links.send(r, r, t) for t in (right, left, across)]
+        yield
+        for step in range(4):
+            for c in s:
+                c.wait_recv()
+            s = []
+            for sign, t, half in ((-1, up, 0), (1, down, NX // 2)):
+                xs = pl.ds(0, NX) if step < 3 else pl.ds(half, NX // 2)
+                r = w.at[ry(y + sign * step), xs, k, :, A]
+                s.append(links.send(r, r, t))
+            yield
+        for c in s:
+            c.wait_recv()
+
+    def seq_b(k):
+        s = []
+        for step in range(4):
+            for c in s:
+                c.wait_recv()
+            s = []
+            for sign, t, half in ((-1, up, pl.ds(CA, CH)), (1, down, pl.ds(CA + CH, CB - CH))):
+                r = w.at[ry(y + sign * step), x, k, :, B if step < 3 else half]
+                s.append(links.send(r, r, t))
+            yield
+        for c in s:
+            c.wait_recv()
+        r = w.at[:, x, k, :, B]
+        s = [links.send(r, r, t) for t in (right, left)]
+        yield
+        for c in s:
+            c.wait_recv()
+        s = []
+        for d, t, h in ((-1, right, 0), (1, left, NY // 2)):
+            r = w.at[pl.ds(h, NY // 2), rx(x + d), k, :, B]
+            s.append(links.send(r, r, t))
+        yield
+        for c in s:
+            c.wait_recv()
+
+    def seq(d):
+        if d:
+            yield
+            far[d - 1].wait_recv()
+        k = rz(z - d)
+        yield from rounds([seq_b(k), seq_a(k)])
+
+    yield from rounds([seq(0), seq(1), seq(2)])
+
+
+N_GATHER = 2 + 3 * (3 + 8 + 8 + 4)
+N_SCATTER = 2 + 3 * (3 + 8 + 8 + 4) + 1
+SCATTER_LANDING = [
+    pltpu.VMEM((NZ, 2, 4, NX, 8, CA), BF),
+    pltpu.VMEM((NZ, 3, 8, CA), BF),
+    pltpu.VMEM((NZ, 2, NY // 2, 8, CB), BF),
+    pltpu.VMEM((NZ, 2, NY, 8, CB), BF),
+    pltpu.VMEM((NZ, 2, 4, 8, CB), BF),
+    pltpu.VMEM((2, 8, D), BF),
+]
+
+
+def scatter_rows(links, g, landing, y, x, z, head):
+    lay, lax_, lbx1, lbx2, lby, lz = landing
+    up, down = at(y + 1, x, z, head), at(y - 1, x, z, head)
+    right, left, across = (at(y, x + d, z, head) for d in (1, -1, 2))
+
+    def add(here, *theirs):
+        total = g[here].astype(F32)
+        for ref, idx in theirs:
+            total = total + ref[idx].astype(F32)
+        g[here] = total.astype(BF)
+
+    rows = slice(None)
+
+    def seq_a(k):
+        s = []
+        for step in range(4):
+            n = []
+            for i, (sign, t) in enumerate(((1, up), (-1, down))):
+                slab = ry(y + sign * (4 - step))
+                half = pl.ds(i * (NX // 2), NX // 2)
+                if step:
+                    s[i].wait_recv()
+                    xs = half if step == 1 else pl.ds(0, NX)
+                    add((slab, xs, k, rows, A), (lay, (k, i, step - 1, xs)))
+                xs = half if step == 0 else pl.ds(0, NX)
+                n.append(links.send(g.at[slab, xs, k, :, A], lay.at[k, i, step, xs], t))
+            s = n
+            yield
+        for c in s:
+            c.wait_recv()
+        add((y, pl.ds(0, NX), k, rows, A), (lay, (k, 0, 3)), (lay, (k, 1, 3)))
+        s = [links.send(g.at[y, rx(x + d), k, :, A], lax_.at[k, d - 1], t)
+             for d, t in ((1, right), (2, across), (3, left))]
+        yield
+        for c in s:
+            c.wait_recv()
+        add((y, x, k, rows, A), (lax_, (k, 0)), (lax_, (k, 1)), (lax_, (k, 2)))
+
+    def seq_b(k):
+        s = []
+        for i, t in enumerate((right, left)):
+            ys = pl.ds(i * (NY // 2), NY // 2)
+            s.append(links.send(g.at[ys, rx(x + 2), k, :, B], lbx1.at[k, i], t))
+        yield
+        n = []
+        for i, (sign, t) in enumerate(((1, right), (-1, left))):
+            ys = pl.ds(i * (NY // 2), NY // 2)
+            s[i].wait_recv()
+            add((ys, rx(x + sign), k, rows, B), (lbx1, (k, i)))
+            n.append(links.send(g.at[:, rx(x + sign), k, :, B], lbx2.at[k, i], t))
+        yield
+        for c in n:
+            c.wait_recv()
+        add((pl.ds(0, NY), x, k, rows, B), (lbx2, (k, 0)), (lbx2, (k, 1)))
+        s = []
+        halves = (pl.ds(0, CH), pl.ds(CH, CB - CH))
+        for step in range(4):
+            n = []
+            for i, (sign, t) in enumerate(((1, up), (-1, down))):
+                slab = ry(y + sign * (4 - step))
+                if step:
+                    s[i].wait_recv()
+                    h = halves[i] if step == 1 else pl.ds(0, CB)
+                    add((slab, x, k, rows, pl.ds(CA + h.start, h.size)), (lby, (k, i, step - 1, rows, h)))
+                h = pl.ds(0, CB) if step else halves[i]
+                n.append(links.send(g.at[slab, x, k, :, pl.ds(CA + h.start, h.size)], lby.at[k, i, step, :, h], t))
+            s = n
+            yield
+        for c in s:
+            c.wait_recv()
+        add((y, x, k, rows, B), (lby, (k, 0, 3)), (lby, (k, 1, 3)))
+
+    sent = []
+
+    def seq(d):
+        k = rz(z + d)
+        yield from rounds([seq_b(k), seq_a(k)])
+        if d:
+            sent.append(links.send(g.at[y, x, k], lz.at[d - 1], at(y, x, k, head)))
+
+    yield from rounds([seq(1), seq(2), seq(0)])
+    for c in sent:
+        c.wait_recv()
+    yield
+
+
+WHOLE = pl.BlockSpec(memory_space=pltpu.VMEM)
+BLOCKS = (NY, NX, NZ, 8, D)
+
+
+def gather_kernel(w_ref, o_ref, w, send_sem, recv_sem):
+    y, x, z, head = places()
+    w[y, x, z] = w_ref[0]
+    enter(peers(y, x, z, head))
+    links = Links(send_sem, recv_sem)
+    for _ in gather_rows(links, w, y, x, z, head):
+        pass
+    links.finish()
+    o_ref[...] = w[...]
+
+
+def gather_weights(w):
+    return pl.pallas_call(
+        gather_kernel,
+        out_shape=jax.ShapeDtypeStruct(BLOCKS, BF),
+        in_specs=[WHOLE],
+        out_specs=WHOLE,
+        scratch_shapes=[
+            pltpu.VMEM(BLOCKS, BF),
+            pltpu.SemaphoreType.DMA((N_GATHER,)),
+            pltpu.SemaphoreType.DMA((N_GATHER,)),
+        ],
+        compiler_params=pltpu.CompilerParams(
+            collective_id=1, has_side_effects=True, vmem_limit_bytes=40 << 20
+        ),
+        name="gather_weights",
+    )(w)
+
+
+def scatter_kernel(g_ref, o_ref, *scratch):
+    g, landing = scratch[0], scratch[1:7]
+    pair_out, pair_in, send_sem, recv_sem = scratch[7:]
+    y, x, z, head = places()
+    dp = lax.axis_index("dp")
+    sibling = (dp, head + 1 - 2 * (head % 2))
+    enter(peers(y, x, z, head) + [sibling])
+    g[...] = g_ref[...]
+    links = Links(send_sem, recv_sem)
+    for _ in scatter_rows(links, g, landing, y, x, z, head):
+        pass
+    own = g[y, x, z].astype(F32) + landing[5][0].astype(F32) + landing[5][1].astype(F32)
+    pair_out[...] = own.astype(BF)
+    links.send(pair_out, pair_in, sibling).wait_recv()
+    shared = dp * 8 >= QH_DEV * HD
+    o_ref[0] = own + jnp.where(shared, pair_in[...].astype(F32), 0.0)
+    links.finish()
+
+
+def scatter_grads(g):
+    return pl.pallas_call(
+        scatter_kernel,
+        out_shape=jax.ShapeDtypeStruct((1, 8, D), F32),
+        in_specs=[WHOLE],
+        out_specs=WHOLE,
+        scratch_shapes=[
+            pltpu.VMEM(BLOCKS, BF),
+            *SCATTER_LANDING,
+            pltpu.VMEM((8, D), BF),
+            pltpu.VMEM((8, D), BF),
+            pltpu.SemaphoreType.DMA((N_SCATTER,)),
+            pltpu.SemaphoreType.DMA((N_SCATTER,)),
+        ],
+        compiler_params=pltpu.CompilerParams(
+            collective_id=2, has_side_effects=True, vmem_limit_bytes=40 << 20
+        ),
+        name="scatter_grads",
+    )(g)
+
+
 def from_behind(x, axis, by):
     devices = lax.axis_size(axis)
     pairs = [(i, i + by) for i in range(devices) if 0 <= i + by < devices]
     return lax.ppermute(x, axis, pairs)
-
-
-def partner(x, axis, apart):
-    return lax.ppermute(x, axis, [(i, i ^ 1 << apart) for i in range(lax.axis_size(axis))])
 
 
 def rope_tables(position, head_size):
@@ -100,7 +404,7 @@
     position = block_index * ROWS + jnp.arange(ROWS, dtype=jnp.int32)
     key_place = (block_index - SPAN) * ROWS + jnp.arange((SPAN + 1) * ROWS, dtype=jnp.int32)
     cosine_table, sine_table = rope_tables(position, HD)
-    weight_piece = lax.all_gather(weights, "dp", axis=1, tiled=True)
+    weight_piece = gather_weights(weights).reshape(1, COLS, D)
     projected = jnp.einsum("rd,cd->rc", tokens, weight_piece[0], preferred_element_type=jnp.float32)
     prepared, pullback = jax.vjp(
         lambda values: prepare(values, query_gain, key_gain, cosine_table, sine_table), projected
@@ -128,18 +432,9 @@
     token_grad = lax.psum_scatter(
         partial_grad.astype(jnp.bfloat16), "head", scatter_dimension=1, tiled=True
     )
-    shard_rows = COLS // lax.axis_size("dp")
-    own_grad = lax.psum_scatter(
-        jnp.einsum("rc,rd->cd", grad_projected, tokens, preferred_element_type=jnp.float32),
-        "dp",
-        scatter_dimension=0,
-        tiled=True,
-    )
-    partner_grad = partner(own_grad.astype(jnp.bfloat16), "head", 0).astype(own_grad.dtype)
-    global_rows = block_index * shard_rows + jnp.arange(shard_rows, dtype=jnp.int32)
-    shared_rows = global_rows >= QH_DEV * HD
-    weight_grad = jnp.where(shared_rows[:, None], own_grad + partner_grad, own_grad)
-    return (attended.reshape(ROWS, QH_DEV * HD), token_grad, weight_grad[None])
+    own_grad = jnp.einsum("rc,rd->cd", grad_projected, tokens, preferred_element_type=jnp.float32)
+    weight_grad = scatter_grads(own_grad.astype(jnp.bfloat16).reshape(BLOCKS))
+    return (attended.reshape(ROWS, QH_DEV * HD), token_grad, weight_grad)
 
 
 def solution(mesh):

time: 972 us -> 171 us (0.18)
  waiting for transfers between devices: 829 us -> 9.4 us
  Pallas kernels: 0 us -> 107 us
  starting transfers between devices: 94 us -> 12.6 us
    reduce_scatter x1 -> x0, waiting for transfers between devices: 613 us -> none  [body(): lax.psum_scatter(jnp.einsum('rc,rd->cd', grad_projected, tokens, preferre...]
    all_gather x1 -> x0, waiting for transfers between devices: 173 us -> none  [body(): weight_piece = lax.all_gather(weights, 'dp', axis=1, tiled=True)]
    pallas_call x0 -> x2, Pallas kernels: none -> 107 us  [the longest x1 60.5 us: scatter_grads(): pl.pallas_call(scatter_kernel, out_shape=jax.ShapeDtypeStruct((1, 8, D),...]
    ppermute x1 -> x0, starting transfers between devices: 79.2 us -> none  [partner(): lax.ppermute(x, axis, [(i, i ^ 1 << apart) for i in range(lax.axis_size(a...]
    reduce_scatter x1, waiting for transfers between devices: 27.9 us -> 0.02 us  [body(): lax.psum_scatter(partial_grad.astype(jnp.bfloat16), 'head', scatter_dimen...]
  transfers between devices with their start and end apart: 8 -> 5, of which waited for: 5 -> 2; matrix products, arithmetic and copies ran while one was open for 1% -> 5% of each run, Pallas kernels for 0% -> 36%
where the time goes in v1:
time: 171 us; the launch traced here: 170 us
  Pallas kernels  107 us (63%)
  between operations  14.4 us (8%)
  starting transfers between devices  12.6 us (7%)
  matrix products  10.3 us (6%)
  waiting for transfers between devices  9.4 us (5%)
  other arithmetic  8.36 us (5%)
  local copies, waits for them, and re-layouts  8.3 us (5%)
    pallas_call x1, Pallas kernels, scatter_grads(): pl.pallas_call(scatter_kernel, out_shape=jax.ShapeDtypeStruct((1, 8, D),...  60.5 us
    pallas_call x1, Pallas kernels, gather_weights(): pl.pallas_call(gather_kernel, out_shape=jax.ShapeDtypeStruct(BLOCKS, BF),...  46.3 us
    ppermute x4, starting transfers between devices, from_behind(): return lax.ppermute(x, axis, pairs)  12.6 us
    ppermute x4, waiting for transfers between devices, from_behind(): return lax.ppermute(x, axis, pairs)  9.36 us
    unnamed x21, local copies, waits for them, and re-layouts  5.77 us
  transfers between devices with their start and end apart: 5, of which 2 were waited for; matrix products, arithmetic and copies ran while one was open for 5% of the time, Pallas kernels for 36%

profile of v1, /device:TPU:1, one launch (start us, length us, event | category | flops | bytes accessed | tf_op | source)
XLA Modules:
  0.0 170.2 jit_solution(7604763495823997584)
XLA Ops:
  7.3 0.8 copy-done.3
  8.1 46.3 %gather_weights.1 = bf16[8,4,3,8,2048]{4,3,2,1,0:T(8,128)(2,1)S(1)} custom-call(bf16[1,8,2048]{2,1,0:T(8,128)(2,1)S(1)} %copy-done.3), custom_call_target="tpu_custom_call" | custom-call | tf_op jit(solution)/shard_map/gather_weights/pallas_call | solution.py:271
  54.4 1.6 copy-done.1
  56.1 1.0 fusion.44
  57.5 1.3 fusion.31
  59.5 5.7 %collective-permute-start.1 = (bf16[256,256]{1,0:T(8,128)(2,1)}, bf16[256,256]{1,0:T(8,128)(2,1)}, u32[]{:S(2)}, u32[]{:S(2)}) collective-permute-start(bf16[256,256]{1,0:T(8,128)(2,1)} %pad_maximum_fusion.2), channel_id=1, source_target_pairs={{0,8},{8,16},{16,24},{24,32},{32,40},{40,48},{48,56},{56,64},{64,7... | collective-permute-start | bytes 393224 | tf_op jit(solution)/shard_map/ppermute | solution.py:331
  65.2 4.1 %collective-permute-start = (bf16[256,256]{1,0:T(8,128)(2,1)}, bf16[256,256]{1,0:T(8,128)(2,1)}, u32[]{:S(2)}, u32[]{:S(2)}) collective-permute-start(bf16[256,256]{1,0:T(8,128)(2,1)} %pad_maximum_fusion.2), channel_id=1, source_target_pairs={{0,16},{8,24},{16,32},{24,40},{32,48},{40,56},{48,64},{56,72},{64,... | collective-permute-start | bytes 393224 | tf_op jit(solution)/shard_map/ppermute | solution.py:331
  70.7 1.8 %copy.66 = bf16[256,512]{0,1:T(8,128)(2,1)} copy(bf16[256,512]{1,0:T(8,128)(2,1)} %param.11) | data formatting | bytes 524288 | tf_op args[5]
  72.5 1.0 copy.63
  74.0 0.9 compare_and_fusion
  74.9 1.0 maximum_maximum_fusion
  76.0 1.0 fusion.3
  77.0 1.4 multiply_reduce_fusion.1
  78.4 1.1 fusion.12
  79.5 1.5 fusion.1
  83.3 1.3 collective-permute-start.2
  84.5 1.5 collective-permute-start.3
  86.4 6.8 %collective-permute-done.2 = bf16[256,256]{1,0:T(8,128)(2,1)} collective-permute-done((bf16[256,256]{1,0:T(8,128)(2,1)}, bf16[256,256]{1,0:T(8,128)(2,1)}, u32[]{:S(2)}, u32[]{:S(2)}) %collective-permute-start.2) | collective-permute-done | bytes 131104 | tf_op jit(solution)/shard_map/ppermute | solution.py:331
  93.2 2.6 %collective-permute-done.3 = bf16[256,256]{1,0:T(8,128)(2,1)} collective-permute-done((bf16[256,256]{1,0:T(8,128)(2,1)}, bf16[256,256]{1,0:T(8,128)(2,1)}, u32[]{:S(2)}, u32[]{:S(2)}) %collective-permute-start.3) | collective-permute-done | bytes 131104 | tf_op jit(solution)/shard_map/ppermute | solution.py:331
  95.8 1.1 fusion.27
  98.3 2.0 %convolution_convert_fusion.1 = bf16[256,2048]{1,0:T(8,128)(2,1)} fusion(bf16[768,2048]{1,0:T(8,128)(2,1)S(1)} %bitcast.44, f32[256,512]{1,0:T(8,128)S(1)} %copy.87, f32[256,128]{1,0:T(8,128)S(1)} %add_add_fusion.1, f32[256,128]{1,0:T(8,128)S(1)} %get-tuple-element.23), kind=kOutput, calls=%fused_computation.5 | convolution fusion | flops 806420480 | bytes 4980736 | tf_op jit(solution)/shard_map/dot_general | solution.py:431
  100.3 0.8 copy.75
  101.2 1.0 convolution_convert_fusion
  102.2 60.5 %scatter_grads.1 = f32[1,8,2048]{2,1,0:T(8,128)S(1)} custom-call(bf16[8,4,3,8,2048]{4,3,2,1,0:T(8,128)(2,1)S(1)} %bitcast.42), custom_call_target="tpu_custom_call" | custom-call | tf_op jit(solution)/shard_map/scatter_grads/pallas_call | solution.py:308
  (56 shorter events, 7.6 us)
Async XLA Ops:
  7.2 48.9 %copy-start = (bf16[256,2048]{1,0:T(8,128)(2,1)S(1)}, bf16[256,2048]{1,0:T(8,128)(2,1)}, u32[]{:S(2)}) copy-start(bf16[256,2048]{1,0:T(8,128)(2,1)} %param.6) | copy-start | bytes 3145732
  7.2 155.6 %reduce-scatter.2.cloned.1.call-start = ((), (), s32[]{:S(2)}) async-start(), calls=%async_computation.1 | async-start | bytes 1179648 | tf_op jit(solution)/shard_map/reduce_scatter | solution.py:432
  7.2 0.8 copy-start.3
  54.4 1.7 copy-start.1
  54.4 2.8 %copy-start.8 = (f32[128]{0:T(128)S(1)}, f32[128]{0:T(128)}, u32[]{:S(2)}) copy-start(f32[128]{0:T(128)} %param.9) | copy-start | bytes 1540
  57.5 16.2 %copy-start.7 = (f32[128]{0:T(128)S(1)}, f32[128]{0:T(128)}, u32[]{:S(2)}) copy-start(f32[128]{0:T(128)} %param.8) | copy-start | bytes 1540
  59.5 15.5 %collective-permute-start.1 = (bf16[256,256]{1,0:T(8,128)(2,1)}, bf16[256,256]{1,0:T(8,128)(2,1)}, u32[]{:S(2)}, u32[]{:S(2)}) collective-permute-start(bf16[256,256]{1,0:T(8,128)(2,1)} %pad_maximum_fusion.2), channel_id=1, source_target_pairs={{0,8},{8,16},{16,24},{24,32},{32,40},{40,48},{48,56},{56,64},{64,7... | collective-permute-start | bytes 393224 | tf_op jit(solution)/shard_map/ppermute | solution.py:331
  65.2 9.8 %collective-permute-start = (bf16[256,256]{1,0:T(8,128)(2,1)}, bf16[256,256]{1,0:T(8,128)(2,1)}, u32[]{:S(2)}, u32[]{:S(2)}) collective-permute-start(bf16[256,256]{1,0:T(8,128)(2,1)} %pad_maximum_fusion.2), channel_id=1, source_target_pairs={{0,16},{8,24},{16,32},{24,40},{32,48},{40,56},{48,64},{56,72},{64,... | collective-permute-start | bytes 393224 | tf_op jit(solution)/shard_map/ppermute | solution.py:331
  73.8 3.2 %copy-start.6 = (bf16[256,512]{0,1:T(8,128)(2,1)S(1)}, bf16[256,512]{0,1:T(8,128)(2,1)}, u32[]{:S(2)}) copy-start(bf16[256,512]{0,1:T(8,128)(2,1)} %copy.66) | copy-start | bytes 786436
  79.5 3.0 %copy-start.4 = (f32[768,128]{1,0:T(8,128)}, f32[768,128]{1,0:T(8,128)S(1)}, u32[]{:S(2)}) copy-start(f32[768,128]{1,0:T(8,128)S(1)} %fusion.12) | copy-start | bytes 1179652
  83.3 9.9 %collective-permute-start.2 = (bf16[256,256]{1,0:T(8,128)(2,1)}, bf16[256,256]{1,0:T(8,128)(2,1)}, u32[]{:S(2)}, u32[]{:S(2)}) collective-permute-start(bf16[256,256]{1,0:T(8,128)(2,1)} %get-tuple-element.21), channel_id=1, source_target_pairs={{8,0},{16,8},{24,16},{32,24},{40,32},{48,40},{56,48},{64,56},{72,6... | collective-permute-start | bytes 393224 | tf_op jit(solution)/shard_map/ppermute | solution.py:331
  84.5 11.2 %collective-permute-start.3 = (bf16[256,256]{1,0:T(8,128)(2,1)}, bf16[256,256]{1,0:T(8,128)(2,1)}, u32[]{:S(2)}, u32[]{:S(2)}) collective-permute-start(bf16[256,256]{1,0:T(8,128)(2,1)} %get-tuple-element.22), channel_id=1, source_target_pairs={{16,0},{24,8},{32,16},{40,24},{48,32},{56,40},{64,48},{72,56},{80,... | collective-permute-start | bytes 393224 | tf_op jit(solution)/shard_map/ppermute | solution.py:331
  86.4 11.8 %copy-start.2 = (bf16[8,4,3,8,2048]{4,3,2,1,0:T(8,128)(2,1)S(1)}, bf16[8,4,3,8,2048]{4,3,2,1,0:T(8,128)(2,1)}, u32[]{:S(2)}) copy-start(bf16[8,4,3,8,2048]{4,3,2,1,0:T(8,128)(2,1)} %copy-done.1) | copy-start | bytes 9437188
  98.3 2.0 %copy-start.5 = (bf16[256,4,128]{0,2,1:T(8,128)(2,1)S(1)}, bf16[256,4,128]{0,2,1:T(8,128)(2,1)}, u32[]{:S(2)}) copy-start(bf16[256,4,128]{0,2,1:T(8,128)(2,1)} %get-tuple-element.35) | copy-start | bytes 786436
Sparse Core Ops, SparseCore 0:
  100.4 57.1 reduce-scatter.1

commit v2 on v1

v2 whole, which is shorter than its diff:
```python
import math

import jax
import jax.numpy as jnp
import numpy as np
from jax import lax
from jax.experimental import pallas as pl
from jax.experimental.pallas import tpu as pltpu
from jax.sharding import PartitionSpec as P

HD = 128
QH_DEV = 4
QC = QH_DEV * HD
COLS = 768
ROWS = 256
SPAN = 2
N_DP = 96
N_LOW = 4
HALF = HD // 2


EPSILON = 1e-06
THETA = 1000000.0
STRETCH = 0.25
SCALE = 1.0 / math.sqrt(HD)


NY, NX, NZ = 8, 4, 3
D = 2048
CA = 896
CB = D - CA
CH = CB // 256 * 128
MESH = pl.DeviceIdType.MESH
BF, F32 = jnp.bfloat16, jnp.float32


class Links:
    def __init__(self, send_sem, recv_sem):
        self.send_sem, self.recv_sem = send_sem, recv_sem
        self.sent = []

    def send(self, src, dst, target):
        n = len(self.sent)
        copy = pltpu.make_async_remote_copy(
            src_ref=src, dst_ref=dst, send_sem=self.send_sem.at[n], recv_sem=self.recv_sem.at[n],
            device_id=target, device_id_type=MESH)
        copy.start()
        self.sent.append(copy)
        return copy

    def finish(self):
        for copy in self.sent:
            copy.wait_send()


def rounds(sequences):
    live = list(sequences)
    while live:
        still = []
        for s in live:
            if next(s, 0) is None:
                still.append(s)
        live = still
        yield


def places():
    dp, head = lax.axis_index("dp"), lax.axis_index("head")
    return dp // (NX * NZ), (dp // NZ) % NX, dp % NZ, head


def at(y, x, z, head):
    return (((y + NY) % NY * NX + (x + NX) % NX) * NZ + (z + NZ) % NZ, head)


def ry(y):
    return (y + NY) % NY


def rx(x):
    return (x + NX) % NX


def rz(z):
    return (z + NZ) % NZ


def peers(y, x, z, head):
    out = [at(y + 1, x, z, head), at(y - 1, x, z, head)]
    out += [at(y, x + d, z, head) for d in (1, 2, 3)]
    out += [at(y, x, z + d, head) for d in (1, 2)]
    return out


def enter(targets):
    barrier = pltpu.get_barrier_semaphore()
    for t in targets:
        pl.semaphore_signal(barrier, inc=1, device_id=t, device_id_type=MESH)
    pl.semaphore_wait(barrier, len(targets))


A = pl.ds(0, CA)
B = pl.ds(CA, CB)


def gather_rows(links, w, y, x, z, head):
    up, down = at(y + 1, x, z, head), at(y - 1, x, z, head)
    right, left, across = (at(y, x + d, z, head) for d in (1, -1, 2))
    own = w.at[y, x, z]
    far = [links.send(own, own, at(y, x, z + d, head)) for d in (1, 2)]

    def seq_a(k):
        r = w.at[y, x, k, :, A]
        s = [links.send(r, r, t) for t in (right, left, across)]
        yield
        for step in range(4):
            for c in s:
                c.wait_recv()
            s = []
            for sign, t, half in ((-1, up, 0), (1, down, NX // 2)):
                xs = pl.ds(0, NX) if step < 3 else pl.ds(half, NX // 2)
                r = w.at[ry(y + sign * step), xs, k, :, A]
                s.append(links.send(r, r, t))
            yield
        for c in s:
            c.wait_recv()

    def seq_b(k):
        s = []
        for step in range(4):
            for c in s:
                c.wait_recv()
            s = []
            for sign, t, half in ((-1, up, pl.ds(CA, CH)), (1, down, pl.ds(CA + CH, CB - CH))):
                r = w.at[ry(y + sign * step), x, k, :, B if step < 3 else half]
                s.append(links.send(r, r, t))
            yield
        for c in s:
            c.wait_recv()
        r = w.at[:, x, k, :, B]
        s = [links.send(r, r, t) for t in (right, left)]
        yield
        for c in s:
            c.wait_recv()
        s = []
        for d, t, h in ((-1, right, 0), (1, left, NY // 2)):
            r = w.at[pl.ds(h, NY // 2), rx(x + d), k, :, B]
            s.append(links.send(r, r, t))
        yield
        for c in s:
            c.wait_recv()

    def seq(d):
        if d:
            yield
            far[d - 1].wait_recv()
        k = rz(z - d)
        yield from rounds([seq_b(k), seq_a(k)])

    yield from rounds([seq(0), seq(1), seq(2)])


N_GATHER = 2 + 3 * (3 + 8 + 8 + 4)
N_SCATTER = 2 + 3 * (3 + 8 + 8 + 4)
SCATTER_LANDING = [
    pltpu.VMEM((NZ, 2, 4, NX, 8, CA), BF),
    pltpu.VMEM((NZ, 3, 8, CA), BF),
    pltpu.VMEM((NZ, 2, NY // 2, 8, CB), BF),
    pltpu.VMEM((NZ, 2, NY, 8, CB), BF),
    pltpu.VMEM((NZ, 2, 4, 8, CB), BF),
    pltpu.VMEM((2, 8, D), BF),
]


def scatter_rows(links, g, landing, y, x, z, head):
    lay, lax_, lbx1, lbx2, lby, lz = landing
    up, down = at(y + 1, x, z, head), at(y - 1, x, z, head)
    right, left, across = (at(y, x + d, z, head) for d in (1, -1, 2))

    def add(here, *theirs):
        total = g[here].astype(F32)
        for ref, idx in theirs:
            total = total + ref[idx].astype(F32)
        g[here] = total.astype(BF)

    rows = slice(None)

    def seq_a(k):
        s = []
        for step in range(4):
            n = []
            for i, (sign, t) in enumerate(((1, up), (-1, down))):
                slab = ry(y + sign * (4 - step))
                half = pl.ds(i * (NX // 2), NX // 2)
                if step:
                    s[i].wait_recv()
                    xs = half if step == 1 else pl.ds(0, NX)
                    add((slab, xs, k, rows, A), (lay, (k, i, step - 1, xs)))
                xs = half if step == 0 else pl.ds(0, NX)
                n.append(links.send(g.at[slab, xs, k, :, A], lay.at[k, i, step, xs], t))
            s = n
            yield
        for c in s:
            c.wait_recv()
        add((y, pl.ds(0, NX), k, rows, A), (lay, (k, 0, 3)), (lay, (k, 1, 3)))
        s = [links.send(g.at[y, rx(x + d), k, :, A], lax_.at[k, d - 1], t)
             for d, t in ((1, right), (2, across), (3, left))]
        yield
        for c in s:
            c.wait_recv()
        add((y, x, k, rows, A), (lax_, (k, 0)), (lax_, (k, 1)), (lax_, (k, 2)))

    def seq_b(k):
        s = []
        for i, t in enumerate((right, left)):
            ys = pl.ds(i * (NY // 2), NY // 2)
            s.append(links.send(g.at[ys, rx(x + 2), k, :, B], lbx1.at[k, i], t))
        yield
        n = []
        for i, (sign, t) in enumerate(((1, right), (-1, left))):
            ys = pl.ds(i * (NY // 2), NY // 2)
            s[i].wait_recv()
            add((ys, rx(x + sign), k, rows, B), (lbx1, (k, i)))
            n.append(links.send(g.at[:, rx(x + sign), k, :, B], lbx2.at[k, i], t))
        yield
        for c in n:
            c.wait_recv()
        add((pl.ds(0, NY), x, k, rows, B), (lbx2, (k, 0)), (lbx2, (k, 1)))
        s = []
        halves = (pl.ds(0, CH), pl.ds(CH, CB - CH))
        for step in range(4):
            n = []
            for i, (sign, t) in enumerate(((1, up), (-1, down))):
                slab = ry(y + sign * (4 - step))
                if step:
                    s[i].wait_recv()
                    h = halves[i] if step == 1 else pl.ds(0, CB)
                    add((slab, x, k, rows, pl.ds(CA + h.start, h.size)), (lby, (k, i, step - 1, rows, h)))
                h = pl.ds(0, CB) if step else halves[i]
                n.append(links.send(g.at[slab, x, k, :, pl.ds(CA + h.start, h.size)], lby.at[k, i, step, :, h], t))
            s = n
            yield
        for c in s:
            c.wait_recv()
        add((y, x, k, rows, B), (lby, (k, 0, 3)), (lby, (k, 1, 3)))

    sent = []

    def seq(d):
        k = rz(z + d)
        yield from rounds([seq_b(k), seq_a(k)])
        if d:
            sent.append(links.send(g.at[y, x, k], lz.at[d - 1], at(y, x, k, head)))

    yield from rounds([seq(1), seq(2), seq(0)])
    for c in sent:
        c.wait_recv()
    yield

WHOLE = pl.BlockSpec(memory_space=pltpu.VMEM)
BLOCKS = (NY, NX, NZ, 8, D)
N_COPIES = N_GATHER + N_SCATTER + 4 + 5 + 7 + 1


def dot(a, b):
    return jnp.dot(a, b, preferred_element_type=F32)


def head_rows(h):
    return pl.ds(pl.multiple_of(h * HD, HD), HD)


def normalize(u, gain):
    factor = lax.rsqrt(jnp.mean(u * u, axis=0, keepdims=True) + EPSILON)
    return u * factor, factor


def rotate(n, cos, sin):
    a, b = n[:HALF], n[HALF:]
    return jnp.concatenate([a * cos - b * sin, b * cos + a * sin], axis=0)


def normalize_rotate_back(u, gain, cos, sin, grad):
    n, factor = normalize(u, gain)
    a, b = grad[:HALF], grad[HALF:]
    back = jnp.concatenate([a * cos + b * sin, b * cos - a * sin], axis=0) * gain
    return factor * (back - n * jnp.mean(back * n, axis=0, keepdims=True))


def layer_kernel(
    tokens,
    w_ref,
    query_gain,
    key_gain,
    frequency,
    first_row,
    cotangent,
    attended,
    token_grad,
    weight_grad,
    w,
    g,
    *scratch,
):
    landing, scratch = scratch[:6], scratch[6:]
    (
        pair_out, pair_in, tokens_t, cot_t, tables, gains, proj_t, q_t, q_n, kv_t, kv_n, weight, denom,
        att_t, dq_t, dkv, d_out, d_pair, d_sum, d_in, gq_t, gq_n, part, tp, tp_pair, tp_low, send_sem, recv_sem,
    ) = scratch
    dp = lax.axis_index("dp")
    y, x, z, head = places()
    low, core = head // 2, head % 2
    other = 1 - core
    sibling = (dp, 2 * low + other)
    ahead = [((dp + d) % N_DP, head) for d in (1, 2)]
    behind = [((dp + N_DP - d) % N_DP, head) for d in (1, 2)]
    lows = [(dp, (low + d) % N_LOW * 2 + core) for d in (1, 2, 3)]
    w[y, x, z] = w_ref[0]
    enter(peers(y, x, z, head) + [sibling] + ahead + behind + lows)
    links = Links(send_sem, recv_sem)
    w2, g2 = w.reshape(COLS, D), g.reshape(COLS, D)

    gather = gather_rows(links, w, y, x, z, head)
    next(gather)
    for c in range(0, D, ROWS):
        tokens_t[pl.ds(c, ROWS)] = tokens[:, pl.ds(c, ROWS)].T
    next(gather)
    cot_t[...] = cotangent[...].T
    square = (HD, HD)
    gains[0] = jnp.broadcast_to(query_gain[...], square).T
    gains[1] = jnp.broadcast_to(key_gain[...], square).T
    rate = jnp.broadcast_to(frequency[...], square).T[:HALF]
    rate = jnp.concatenate([rate, rate], axis=1)
    place = (dp * ROWS + lax.broadcasted_iota(jnp.int32, (HALF, ROWS), 1)).astype(F32)
    angles = place * STRETCH * rate
    tables[0] = jnp.cos(angles)
    tables[1] = jnp.sin(angles)
    for _ in gather:
        pass

    def project(h, _):
        proj_t[head_rows(h)] = dot(w2[head_rows(h)], tokens_t[...])
        return 0

    lax.fori_loop(0, COLS // HD, project, 0)

    def gain_of(i):
        return jnp.concatenate([gains[i], gains[i]], axis=1)

    def prepared(h, i):
        n, _ = normalize(proj_t[head_rows(h)], None)
        return rotate(n * gain_of(i), tables[0], tables[1]).astype(BF)

    kv_t[0, 0] = prepared(QH_DEV, 1)
    kv_t[0, 1] = proj_t[pl.ds(QC + HD, HD)].astype(BF)
    halo = [links.send(kv_t.at[0, core], kv_t.at[d, core], ahead[d - 1]) for d in (1, 2)]

    def natural(j):
        kv_n[j, 0] = kv_t[j, 0].T
        kv_n[j, 1] = kv_t[j, 1].T

    natural(0)

    def prepare_query(h, _):
        turned = prepared(h, 0)
        q_t[head_rows(h)] = turned
        q_n[h] = turned.T
        return 0

    lax.fori_loop(0, QH_DEV, prepare_query, 0)

    row = lax.broadcasted_iota(jnp.int32, (ROWS, ROWS), 1)
    key = lax.broadcasted_iota(jnp.int32, (ROWS, ROWS), 0)

    def forward(j, h):
        key_place = (dp - j) * ROWS + key
        visible = key_place >= first_row[...]
        if j == 0:
            visible = visible & (key <= row)
        score = dot(kv_n[j, 0], q_t[head_rows(h)]) * SCALE
        seen = jnp.where(visible, jnp.exp(score), 0.0)
        weight[h, j] = seen
        return jnp.sum(seen, axis=0, keepdims=True), dot(kv_t[j, 1], seen.astype(BF))

    def own_forward(h, _):
        denom[h], att_t[head_rows(h)] = forward(0, h)
        return 0

    lax.fori_loop(0, QH_DEV, own_forward, 0)

    pair = []
    for d in (1, 2):
        halo[d - 1].wait_recv()
        pair.append(links.send(kv_t.at[d, core], kv_t.at[d, core], sibling))
    for d in (1, 2):
        pair[d - 1].wait_recv()
        natural(d)

    def backward(j, h, inverse, delta):
        probability = weight[h, j] * inverse
        grad_prob = dot(kv_n[j, 1], cot_t[head_rows(h)])
        grad_score = (probability * (grad_prob - delta) * SCALE).astype(BF)
        dk = dot(grad_score, q_n[h])
        dv = dot(probability.astype(BF), cotangent[:, head_rows(h)])
        return dot(kv_t[j, 0], grad_score), dk, dv

    dkv[...] = jnp.zeros_like(dkv)

    def far(h, _):
        total, summed = denom[h], att_t[head_rows(h)]
        for j in (1, 2):
            more, moved = forward(j, h)
            total = total + more
            summed = summed + moved
        inverse = 1.0 / total
        out = (summed * inverse).astype(BF)
        attended[:, head_rows(h)] = out.T
        delta = jnp.sum(cot_t[head_rows(h)].astype(F32) * out.astype(F32), axis=0, keepdims=True)
        denom[h] = inverse
        att_t[head_rows(h)] = jnp.broadcast_to(delta, (HD, ROWS))
        dq = None
        for j in (1, 2):
            more, dk, dv = backward(j, h, inverse, delta)
            dq = more if dq is None else dq + more
            dkv[j, 0] += dk
            dkv[j, 1] += dv
        dq_t[head_rows(h)] = dq
        return 0

    lax.fori_loop(0, QH_DEV, far, 0)

    def to_pair(j):
        d_out[j] = dkv[j, other].astype(BF)
        return links.send(d_out.at[j], d_pair.at[j], sibling)

    back = [to_pair(j) for j in (1, 2)]

    def near(h, _):
        dq, dk, dv = backward(0, h, denom[h], att_t[pl.ds(pl.multiple_of(h * HD, HD), 8)][:1])
        dkv[0, 0] += dk
        dkv[0, 1] += dv
        grad = dq_t[head_rows(h)] + dq
        back_t = normalize_rotate_back(proj_t[head_rows(h)], gain_of(0), tables[0], tables[1], grad).astype(BF)
        gq_t[head_rows(h)] = back_t
        gq_n[:, head_rows(h)] = back_t.T
        return 0

    for j in (1, 2):
        back[j - 1].wait_recv()
        d_sum[j - 1] = (dkv[j, core] + d_pair[j].astype(F32)).astype(BF)
        back[j - 1] = links.send(d_sum.at[j - 1], d_in.at[j - 1], behind[j - 1])
    lax.fori_loop(0, QH_DEV, near, 0)
    back_own = to_pair(0)

    def own_grads(h, _):
        g2[head_rows(h)] = dot(gq_t[head_rows(h)], tokens[...]).astype(BF)
        return 0

    lax.fori_loop(0, QH_DEV, own_grads, 0)
    mine = pl.ds(pl.multiple_of(QC + core * HD, HD), HD)
    theirs = pl.ds(pl.multiple_of(QC + other * HD, HD), HD)
    g2[theirs] = jnp.zeros((HD, D), BF)

    def token_part(i, _):
        cols = pl.ds(pl.multiple_of(i * ROWS, ROWS), ROWS)
        part[i] = dot(gq_n[...], w2[pl.ds(0, QC), cols])
        return 0

    lax.fori_loop(0, 8, token_part, 0)

    back_own.wait_recv()
    total = dkv[0, core] + d_pair[0].astype(F32)
    for j in (0, 1):
        back[j].wait_recv()
        total = total + d_in[j].astype(F32)
    total = total.T
    turned = normalize_rotate_back(proj_t[pl.ds(QC, HD)], gain_of(1), tables[0], tables[1], total)
    total = jnp.where(core == 0, turned, total).astype(BF)
    gk_n = total.T
    g2[mine] = dot(total, tokens[...]).astype(BF)

    scatter = scatter_rows(links, g, landing, y, x, z, head)
    next(scatter)

    def token_rest(i, _):
        cols = pl.ds(pl.multiple_of(i * ROWS, ROWS), ROWS)
        tp[i] = (part[i] + dot(gk_n, w2[mine, cols])).astype(BF)
        return 0

    lax.fori_loop(0, 8, token_rest, 0)
    swap = [links.send(tp.at[2 * i + other], tp_pair.at[i], sibling) for i in range(N_LOW)]
    next(scatter)
    for i in range(N_LOW):
        swap[i].wait_recv()
        tp[2 * i + core] = (tp[2 * i + core].astype(F32) + tp_pair[i].astype(F32)).astype(BF)
    low_copies = [
        links.send(tp.at[(low + d) % N_LOW * 2 + core], tp_low.at[d - 1], lows[d - 1]) for d in (1, 2, 3)
    ]
    for _ in scatter:
        pass
    own = g[y, x, z].astype(F32) + landing[5][0].astype(F32) + landing[5][1].astype(F32)
    pair_out[...] = own.astype(BF)
    last = links.send(pair_out, pair_in, sibling)
    total = tp[head].astype(F32)
    for d in range(3):
        low_copies[d].wait_recv()
        total = total + tp_low[d].astype(F32)
    token_grad[...] = total.astype(BF)
    last.wait_recv()
    weight_grad[0] = own + jnp.where(dp * 8 >= QC, pair_in[...].astype(F32), 0.0)
    links.finish()


def body(tokens, weights, query_gain, key_gain, first_row, cotangent):
    channel = np.arange(HALF, dtype=np.float64)
    rates = (THETA ** (-2.0 * channel / HD)).astype(np.float32)
    frequency = jnp.asarray(np.concatenate([rates, rates])[None])
    return pl.pallas_call(
        layer_kernel,
        out_shape=(
            jax.ShapeDtypeStruct((ROWS, QC), BF),
            jax.ShapeDtypeStruct((ROWS, D // 8), BF),
            jax.ShapeDtypeStruct((1, 8, D), F32),
        ),
        in_specs=[WHOLE] * 7,
        out_specs=[WHOLE] * 3,
        scratch_shapes=[
            pltpu.VMEM(BLOCKS, BF),
            pltpu.VMEM(BLOCKS, BF),
            *SCATTER_LANDING,
            pltpu.VMEM((8, D), BF),
            pltpu.VMEM((8, D), BF),
            pltpu.VMEM((D, ROWS), BF),
            pltpu.VMEM((QC, ROWS), BF),
            pltpu.VMEM((2, HALF, ROWS), F32),
            pltpu.VMEM((2, HD, HD), F32),
            pltpu.VMEM((COLS, ROWS), F32),
            pltpu.VMEM((QC, ROWS), BF),
            pltpu.VMEM((QH_DEV, ROWS, HD), BF),
            pltpu.VMEM((SPAN + 1, 2, HD, ROWS), BF),
            pltpu.VMEM((SPAN + 1, 2, ROWS, HD), BF),
            pltpu.VMEM((QH_DEV, SPAN + 1, ROWS, ROWS), F32),
            pltpu.VMEM((QH_DEV, 1, ROWS), F32),
            pltpu.VMEM((QC, ROWS), F32),
            pltpu.VMEM((QC, ROWS), F32),
            pltpu.VMEM((SPAN + 1, 2, ROWS, HD), F32),
            pltpu.VMEM((SPAN + 1, ROWS, HD), BF),
            pltpu.VMEM((SPAN + 1, ROWS, HD), BF),
            pltpu.VMEM((SPAN, ROWS, HD), BF),
            pltpu.VMEM((SPAN, ROWS, HD), BF),
            pltpu.VMEM((QC, ROWS), BF),
            pltpu.VMEM((ROWS, QC), BF),
            pltpu.VMEM((8, ROWS, ROWS), F32),
            pltpu.VMEM((8, ROWS, ROWS), BF),
            pltpu.VMEM((N_LOW, ROWS, ROWS), BF),
            pltpu.VMEM((N_LOW - 1, ROWS, ROWS), BF),
            pltpu.SemaphoreType.DMA((N_COPIES,)),
            pltpu.SemaphoreType.DMA((N_COPIES,)),
        ],
        compiler_params=pltpu.CompilerParams(
            collective_id=1, has_side_effects=True, vmem_limit_bytes=50 << 20
        ),
        cost_estimate=pl.CostEstimate(flops=4 * 10**9, bytes_accessed=4 << 20, transcendentals=10**6),
        name="masked_attention_layer",
    )(
        tokens,
        weights,
        query_gain.reshape(1, HD),
        key_gain.reshape(1, HD),
        frequency,
        first_row.reshape(1, ROWS),
        cotangent,
    )


def solution(mesh):
    in_specs = (P("dp", None), P("head", "dp", None), P(), P(), P("dp"), P("dp", "head"))
    out_specs = (P("dp", "head"), P("dp", "head"), P("head", "dp", None))
    return jax.shard_map(body, mesh=mesh, in_specs=in_specs, out_specs=out_specs, check_vma=False)
```

time: 171 us -> 125 us (0.73)
  between operations: 14.4 us -> 0.68 us
  starting transfers between devices: 12.6 us -> 0 us
  matrix products: 10.3 us -> 0 us
  Pallas kernels: 107 us -> 117 us
  waiting for transfers between devices: 9.4 us -> 0 us
  other arithmetic: 8.36 us -> 0 us
  local copies, waits for them, and re-layouts: 8.3 us -> 5.6 us
    ppermute x4 -> x0, starting transfers between devices: 12.6 us -> none  [from_behind(): return lax.ppermute(x, axis, pairs)]
    pallas_call x2 -> x1, Pallas kernels: 107 us -> 117 us  [body(): pl.pallas_call(layer_kernel, out_shape=(jax.ShapeDtypeStruct((ROWS, QC),...]
    dot_general x9 -> x0, matrix products: 10.3 us -> none  [the longest x1 2 us: body(): jnp.dot(grad_projected, weight_piece[0], preferred_element_type=jnp.float32)]
    ppermute x4 -> x0, waiting for transfers between devices: 9.36 us -> none  [from_behind(): return lax.ppermute(x, axis, pairs)]
    unnamed x21 -> x17, local copies, waits for them, and re-layouts: 5.77 us -> 5.6 us
  transfers between devices with their start and end apart: 5 -> 0, of which waited for: 2 -> 0; matrix products, arithmetic and copies ran while one was open for 5% -> 0% of each run, Pallas kernels for 36% -> 0%
where the time goes in v2:
time: 125 us; the launch traced here: 124 us
  Pallas kernels  117 us (94%)
  local copies, waits for them, and re-layouts  5.6 us (4%)
    pallas_call x1, Pallas kernels, body(): pl.pallas_call(layer_kernel, out_shape=(jax.ShapeDtypeStruct((ROWS, QC),...  117 us
    unnamed x17, local copies, waits for them, and re-layouts  5.6 us

profile of v2, /device:TPU:1, one launch (start us, length us, event | category | flops | bytes accessed | tf_op | source)
XLA Modules:
  0.0 123.6 jit_solution(6292313926808218559)
XLA Ops:
  0.6 0.0 copy-start.5
  0.6 0.0 copy-start.6
  0.7 0.0 copy-start.3
  0.7 0.0 copy-start.4
  0.7 0.6 copy-done.5
  1.3 0.0 copy-done.6
  1.3 0.0 copy-done.3
  1.3 0.0 copy-done.4
  1.3 0.0 copy-start
  1.3 1.2 copy-done
  2.6 0.0 copy-start.1
  2.6 0.9 copy-done.1
  3.5 0.0 copy-start.2
  3.5 0.8 copy-done.2
  4.3 117.4 %masked_attention_layer.1 = (bf16[256,512]{1,0:T(8,128)(2,1)S(1)}, bf16[256,256]{1,0:T(8,128)(2,1)S(1)}, f32[1,8,2048]{2,1,0:T(8,128)S(1)}) custom-call(bf16[256,2048]{1,0:T(8,128)(2,1)S(1)} %copy-done, bf16[1,8,2048]{2,1,0:T(8,128)(2,1)S(1)} %copy-done.2, f32[1,128]{1,0:T(1,128)S(1)} %bitcast.4, f32[1,128]{1,0:T(1,128)S(1)} %bitcast.5, ...), custom_call_target="tpu_custom_call" | custom-call | flops 4000000000 | bytes 4194304 | tf_op jit(solution)/shard_map/masked_attention_layer/pallas_call | solution.py:518
  121.7 0.7 copy.13
  122.4 0.7 copy.14
  123.0 0.6 copy.15
Async XLA Ops:
  0.6 0.7 copy-start.5
  0.6 0.7 copy-start.6
  0.7 0.7 copy-start.3
  0.7 0.7 copy-start.4
  1.3 1.2 copy-start
  2.6 0.9 copy-start.1
  3.5 0.8 copy-start.2

commit v3 on v2

--- a/solution.py
+++ b/solution.py
@@ -27,9 +27,9 @@
 
 NY, NX, NZ = 8, 4, 3
 D = 2048
-CA = 896
+CA = 1024
 CB = D - CA
-CH = CB // 256 * 128
+CH = CB // 2
 MESH = pl.DeviceIdType.MESH
 BF, F32 = jnp.bfloat16, jnp.float32
 
@@ -60,8 +60,8 @@
         for s in live:
             if next(s, 0) is None:
                 still.append(s)
+                yield
         live = still
-        yield
 
 
 def places():
@@ -86,7 +86,7 @@
 
 
 def peers(y, x, z, head):
-    out = [at(y + 1, x, z, head), at(y - 1, x, z, head)]
+    out = [at(y + d, x, z, head) for d in (1, -1, 2, -2)]
     out += [at(y, x + d, z, head) for d in (1, 2, 3)]
     out += [at(y, x, z + d, head) for d in (1, 2)]
     return out
@@ -103,89 +103,116 @@
 B = pl.ds(CA, CB)
 
 
+TO_RIGHT = (0, 1, 2, 3)
+
+
 def gather_rows(links, w, y, x, z, head):
-    up, down = at(y + 1, x, z, head), at(y - 1, x, z, head)
+    up, down, up2, down2 = (at(y + d, x, z, head) for d in (1, -1, 2, -2))
     right, left, across = (at(y, x + d, z, head) for d in (1, -1, 2))
     own = w.at[y, x, z]
     far = [links.send(own, own, at(y, x, z + d, head)) for d in (1, 2)]
 
+    def arrived(copies):
+        for c in copies:
+            c.wait_recv()
+
     def seq_a(k):
         r = w.at[y, x, k, :, A]
         s = [links.send(r, r, t) for t in (right, left, across)]
         yield
         for step in range(4):
-            for c in s:
-                c.wait_recv()
+            arrived(s)
             s = []
             for sign, t, half in ((-1, up, 0), (1, down, NX // 2)):
                 xs = pl.ds(0, NX) if step < 3 else pl.ds(half, NX // 2)
                 r = w.at[ry(y + sign * step), xs, k, :, A]
                 s.append(links.send(r, r, t))
             yield
-        for c in s:
-            c.wait_recv()
+        arrived(s)
 
     def seq_b(k):
+        def shard(dy, dx, cols=B):
+            return w.at[ry(y + dy), rx(x + dx), k, :, cols]
+
+        def sideways(dys):
+            out = []
+            for dy in dys:
+                r = shard(dy, 0)
+                out.append((dy, links.send(r, r, right), links.send(r, r, left)))
+            return out
+
+        def onward(came):
+            out = []
+            for dy, from_left, from_right in came:
+                from_left.wait_recv()
+                from_right.wait_recv()
+                r, t = (shard(dy, -1), right) if dy in TO_RIGHT else (shard(dy, 1), left)
+                out.append(links.send(r, r, t))
+            return out
+
+        r = shard(0, 0)
+        s = [links.send(r, r, t) for t in (up, down, up2, down2)]
+        side = sideways((0,))
+        yield
+        arrived(s)
         s = []
-        for step in range(4):
-            for c in s:
-                c.wait_recv()
-            s = []
-            for sign, t, half in ((-1, up, pl.ds(CA, CH)), (1, down, pl.ds(CA + CH, CB - CH))):
-                r = w.at[ry(y + sign * step), x, k, :, B if step < 3 else half]
-                s.append(links.send(r, r, t))
-            yield
-        for c in s:
-            c.wait_recv()
-        r = w.at[:, x, k, :, B]
-        s = [links.send(r, r, t) for t in (right, left)]
-        yield
-        for c in s:
-            c.wait_recv()
-        s = []
-        for d, t, h in ((-1, right, 0), (1, left, NY // 2)):
-            r = w.at[pl.ds(h, NY // 2), rx(x + d), k, :, B]
-            s.append(links.send(r, r, t))
-        yield
-        for c in s:
-            c.wait_recv()
-
-    def seq(d):
+        for dy, t, t2, half in ((-2, up, up2, pl.ds(CA, CH)), (2, down, down2, pl.ds(CA + CH, CH))):
+            r, h = shard(dy, 0), shard(dy, 0, half)
+            s += [links.send(r, r, t), links.send(h, h, t2)]
+        side2 = sideways((2, -2, 1, -1))
+        last = onward(side)
+        yield
+        arrived(s)
+        side3 = sideways((3, -3, 4))
+        last += onward(side2)
+        yield
+        last += onward(side3)
+        yield
+        arrived(last)
+
+    def seq(d, kind):
         if d:
             yield
-            far[d - 1].wait_recv()
-        k = rz(z - d)
-        yield from rounds([seq_b(k), seq_a(k)])
-
-    yield from rounds([seq(0), seq(1), seq(2)])
-
-
-N_GATHER = 2 + 3 * (3 + 8 + 8 + 4)
-N_SCATTER = 2 + 3 * (3 + 8 + 8 + 4)
+            if kind == 0:
+                far[d - 1].wait_recv()
+        yield from (seq_b, seq_a)[kind](rz(z - d))
+
+    yield from rounds([seq(d, kind) for kind in (0, 1) for d in range(NZ)])
+
+
+N_GATHER = 2 + 3 * (11 + 32)
+N_SCATTER = 4 + 3 * (11 + 32)
 SCATTER_LANDING = [
     pltpu.VMEM((NZ, 2, 4, NX, 8, CA), BF),
     pltpu.VMEM((NZ, 3, 8, CA), BF),
-    pltpu.VMEM((NZ, 2, NY // 2, 8, CB), BF),
+    pltpu.VMEM((NZ, NY, 8, CB), BF),
     pltpu.VMEM((NZ, 2, NY, 8, CB), BF),
-    pltpu.VMEM((NZ, 2, 4, 8, CB), BF),
+    pltpu.VMEM((NZ, 8, 8, CB), BF),
     pltpu.VMEM((2, 8, D), BF),
 ]
 
 
 def scatter_rows(links, g, landing, y, x, z, head):
     lay, lax_, lbx1, lbx2, lby, lz = landing
-    up, down = at(y + 1, x, z, head), at(y - 1, x, z, head)
+    up, down, up2, down2 = (at(y + d, x, z, head) for d in (1, -1, 2, -2))
     right, left, across = (at(y, x + d, z, head) for d in (1, -1, 2))
 
     def add(here, *theirs):
-        total = g[here].astype(F32)
+        total = g[here]
         for ref, idx in theirs:
-            total = total + ref[idx].astype(F32)
-        g[here] = total.astype(BF)
+            total = total + ref[idx]
+        g[here] = total
 
     rows = slice(None)
-
-    def seq_a(k):
+    sent = []
+
+    def finish(d, cols):
+        if d:
+            k = rz(z + d)
+            sent.append(links.send(g.at[y, x, k, :, cols], lz.at[d - 1, :, cols], at(y, x, k, head)))
+
+    def seq_a(d):
+        k = rz(z + d)
         s = []
         for step in range(4):
             n = []
@@ -203,61 +230,85 @@
         for c in s:
             c.wait_recv()
         add((y, pl.ds(0, NX), k, rows, A), (lay, (k, 0, 3)), (lay, (k, 1, 3)))
-        s = [links.send(g.at[y, rx(x + d), k, :, A], lax_.at[k, d - 1], t)
-             for d, t in ((1, right), (2, across), (3, left))]
+        s = [links.send(g.at[y, rx(x + e), k, :, A], lax_.at[k, e - 1], t)
+             for e, t in ((1, right), (2, across), (3, left))]
         yield
         for c in s:
             c.wait_recv()
         add((y, x, k, rows, A), (lax_, (k, 0)), (lax_, (k, 1)), (lax_, (k, 2)))
-
-    def seq_b(k):
-        s = []
-        for i, t in enumerate((right, left)):
-            ys = pl.ds(i * (NY // 2), NY // 2)
-            s.append(links.send(g.at[ys, rx(x + 2), k, :, B], lbx1.at[k, i], t))
-        yield
-        n = []
-        for i, (sign, t) in enumerate(((1, right), (-1, left))):
-            ys = pl.ds(i * (NY // 2), NY // 2)
-            s[i].wait_recv()
-            add((ys, rx(x + sign), k, rows, B), (lbx1, (k, i)))
-            n.append(links.send(g.at[:, rx(x + sign), k, :, B], lbx2.at[k, i], t))
+        finish(d, A)
+
+    def seq_b(d):
+        k = rz(z + d)
+
+        def first(dys):
+            out = []
+            for dy in dys:
+                t = right if dy in TO_RIGHT else left
+                out.append((dy, links.send(g.at[ry(y + dy), rx(x + 2), k, :, B], lbx1.at[k, ry(y + dy)], t)))
+            return out
+
+        def second(came):
+            out = []
+            for dy, c in came:
+                ys = ry(y + dy)
+                c.wait_recv()
+                add((ys, rx(x + (1 if dy in TO_RIGHT else -1)), k, rows, B), (lbx1, (k, ys)))
+                out.append((dy, [
+                    links.send(g.at[ys, rx(x + sign), k, :, B], lbx2.at[k, i, ys], t)
+                    for i, (sign, t) in enumerate(((1, right), (-1, left)))
+                ]))
+            return out
+
+        def third(came):
+            for dy, pair in came:
+                ys = ry(y + dy)
+                for c in pair:
+                    c.wait_recv()
+                add((ys, x, k, rows, B), (lbx2, (k, 0, ys)), (lbx2, (k, 1, ys)))
+
+        def toward(dy, slot, t, cols=pl.ds(0, CB)):
+            src = g.at[ry(y + dy), x, k, :, pl.ds(CA + cols.start, cols.size)]
+            return links.send(src, lby.at[k, slot, :, cols], t)
+
+        early, late = (4, 3, -3), (2, -2, 1, -1, 0)
+        s1 = first(early)
+        s2 = first(late)
+        yield
+        s1 = second(s1)
+        yield
+        s2 = second(s2)
+        yield
+        third(s1)
+        h0, h1 = pl.ds(0, CH), pl.ds(CH, CH)
+        s = [toward(3, 0, up), toward(-3, 1, down), toward(4, 2, up2, h0), toward(4, 3, down2, h1)]
+        yield
+        third(s2)
+        n = [toward(1, 4, up), toward(-1, 5, down)]
+        for c in s:
+            c.wait_recv()
+        add((ry(y + 2), x, k, rows, pl.ds(CA, CB)), (lby, (k, 0)))
+        add((ry(y + 2), x, k, rows, pl.ds(CA, CH)), (lby, (k, 2, rows, h0)))
+        add((ry(y - 2), x, k, rows, pl.ds(CA, CB)), (lby, (k, 1)))
+        add((ry(y - 2), x, k, rows, pl.ds(CA + CH, CH)), (lby, (k, 3, rows, h1)))
+        n += [toward(2, 6, up2), toward(-2, 7, down2)]
         yield
         for c in n:
             c.wait_recv()
-        add((pl.ds(0, NY), x, k, rows, B), (lbx2, (k, 0)), (lbx2, (k, 1)))
-        s = []
-        halves = (pl.ds(0, CH), pl.ds(CH, CB - CH))
-        for step in range(4):
-            n = []
-            for i, (sign, t) in enumerate(((1, up), (-1, down))):
-                slab = ry(y + sign * (4 - step))
-                if step:
-                    s[i].wait_recv()
-                    h = halves[i] if step == 1 else pl.ds(0, CB)
-                    add((slab, x, k, rows, pl.ds(CA + h.start, h.size)), (lby, (k, i, step - 1, rows, h)))
-                h = pl.ds(0, CB) if step else halves[i]
-                n.append(links.send(g.at[slab, x, k, :, pl.ds(CA + h.start, h.size)], lby.at[k, i, step, :, h], t))
-            s = n
-            yield
-        for c in s:
-            c.wait_recv()
-        add((y, x, k, rows, B), (lby, (k, 0, 3)), (lby, (k, 1, 3)))
-
-    sent = []
-
-    def seq(d):
-        k = rz(z + d)
-        yield from rounds([seq_b(k), seq_a(k)])
-        if d:
-            sent.append(links.send(g.at[y, x, k], lz.at[d - 1], at(y, x, k, head)))
-
-    yield from rounds([seq(1), seq(2), seq(0)])
+        add((y, x, k, rows, B), *((lby, (k, slot)) for slot in (4, 5, 6, 7)))
+        finish(d, B)
+
+    def late(sequence):
+        yield
+        yield
+        yield from sequence
+
+    yield from rounds([seq_b(1), seq_b(2), seq_a(1), seq_a(2), late(seq_b(0)), late(seq_a(0))])
     for c in sent:
         c.wait_recv()
     yield
 
-WHOLE = pl.BlockSpec(memory_space=pltpu.VMEM)
+
 BLOCKS = (NY, NX, NZ, 8, D)
 N_COPIES = N_GATHER + N_SCATTER + 4 + 5 + 7 + 1
 
@@ -287,25 +338,14 @@
     return factor * (back - n * jnp.mean(back * n, axis=0, keepdims=True))
 
 
-def layer_kernel(
-    tokens,
-    w_ref,
-    query_gain,
-    key_gain,
-    frequency,
-    first_row,
-    cotangent,
-    attended,
-    token_grad,
-    weight_grad,
-    w,
-    g,
-    *scratch,
-):
-    landing, scratch = scratch[:6], scratch[6:]
+def layer_kernel(*refs):
+    hbm_in, hbm_out, (w, g), landing = refs[:7], refs[7:10], refs[10:12], refs[12:18]
+    tokens, query_gain, key_gain, frequency, first_row, cotangent = refs[18:24]
+    results, local_sem, scratch = refs[24:27], refs[27], refs[28:]
+    attended, token_grad, weight_grad = results
     (
         pair_out, pair_in, tokens_t, cot_t, tables, gains, proj_t, q_t, q_n, kv_t, kv_n, weight, denom,
-        att_t, dq_t, dkv, d_out, d_pair, d_sum, d_in, gq_t, gq_n, part, tp, tp_pair, tp_low, send_sem, recv_sem,
+        att_t, dq_t, dkv, d_out, d_pair, d_sum, d_in, gq_t, gq_n, part, tp, tp_pair, tp_low, token_sum, send_sem, recv_sem,
     ) = scratch
     dp = lax.axis_index("dp")
     y, x, z, head = places()
@@ -315,34 +355,58 @@
     ahead = [((dp + d) % N_DP, head) for d in (1, 2)]
     behind = [((dp + N_DP - d) % N_DP, head) for d in (1, 2)]
     lows = [(dp, (low + d) % N_LOW * 2 + core) for d in (1, 2, 3)]
-    w[y, x, z] = w_ref[0]
+    places_in = (tokens, w.at[y, x, z], query_gain, key_gain, frequency, first_row, cotangent)
+    fetch = []
+    for i in (1, 0, 2, 3, 4, 5, 6):
+        source = hbm_in[i].at[0] if i == 1 else hbm_in[i]
+        fetch.append(pltpu.make_async_copy(source, places_in[i], local_sem.at[i]))
+        fetch[-1].start()
+
+    def put(i):
+        copy = pltpu.make_async_copy(results[i], hbm_out[i], local_sem.at[7 + i])
+        copy.start()
+        return copy
+
     enter(peers(y, x, z, head) + [sibling] + ahead + behind + lows)
+    fetch[0].wait()
     links = Links(send_sem, recv_sem)
     w2, g2 = w.reshape(COLS, D), g.reshape(COLS, D)
 
-    gather = gather_rows(links, w, y, x, z, head)
-    next(gather)
-    for c in range(0, D, ROWS):
-        tokens_t[pl.ds(c, ROWS)] = tokens[:, pl.ds(c, ROWS)].T
-    next(gather)
-    cot_t[...] = cotangent[...].T
-    square = (HD, HD)
-    gains[0] = jnp.broadcast_to(query_gain[...], square).T
-    gains[1] = jnp.broadcast_to(key_gain[...], square).T
-    rate = jnp.broadcast_to(frequency[...], square).T[:HALF]
-    rate = jnp.concatenate([rate, rate], axis=1)
-    place = (dp * ROWS + lax.broadcasted_iota(jnp.int32, (HALF, ROWS), 1)).astype(F32)
-    angles = place * STRETCH * rate
-    tables[0] = jnp.cos(angles)
-    tables[1] = jnp.sin(angles)
-    for _ in gather:
+    def prologue():
+        for copy in fetch[1:]:
+            copy.wait()
+        square = (HD, HD)
+        gains[0] = jnp.broadcast_to(query_gain[...], square).T
+        gains[1] = jnp.broadcast_to(key_gain[...], square).T
+        rate = jnp.broadcast_to(frequency[...], square).T[:HALF]
+        rate = jnp.concatenate([rate, rate], axis=1)
+        yield
+        for c in range(0, D, ROWS):
+            tokens_t[pl.ds(c, ROWS)] = tokens[:, pl.ds(c, ROWS)].T
+            yield
+        for c in range(0, QC, ROWS):
+            cot_t[pl.ds(c, ROWS)] = cotangent[:, pl.ds(c, ROWS)].T
+            yield
+        for c in range(0, HALF, 16):
+            place = (dp * ROWS + lax.broadcasted_iota(jnp.int32, (16, ROWS), 1)).astype(F32)
+            angles = place * STRETCH * rate[c : c + 16]
+            tables[0, pl.ds(c, 16)] = jnp.cos(angles)
+            yield
+            tables[1, pl.ds(c, 16)] = jnp.sin(angles)
+            yield
+
+    side = prologue()
+    for i, _ in enumerate(gather_rows(links, w, y, x, z, head)):
+        if i >= 5:
+            next(side, None)
+    for _ in side:
         pass
 
     def project(h, _):
         proj_t[head_rows(h)] = dot(w2[head_rows(h)], tokens_t[...])
         return 0
 
-    lax.fori_loop(0, COLS // HD, project, 0)
+    lax.fori_loop(QH_DEV, COLS // HD, project, 0)
 
     def gain_of(i):
         return jnp.concatenate([gains[i], gains[i]], axis=1)
@@ -360,6 +424,7 @@
         kv_n[j, 1] = kv_t[j, 1].T
 
     natural(0)
+    lax.fori_loop(0, QH_DEV, project, 0)
 
     def prepare_query(h, _):
         turned = prepared(h, 0)
@@ -429,6 +494,8 @@
 
     lax.fori_loop(0, QH_DEV, far, 0)
 
+    put_attended = put(0)
+
     def to_pair(j):
         d_out[j] = dkv[j, other].astype(BF)
         return links.send(d_out.at[j], d_pair.at[j], sibling)
@@ -479,36 +546,51 @@
     gk_n = total.T
     g2[mine] = dot(total, tokens[...]).astype(BF)
 
-    scatter = scatter_rows(links, g, landing, y, x, z, head)
-    next(scatter)
-
-    def token_rest(i, _):
-        cols = pl.ds(pl.multiple_of(i * ROWS, ROWS), ROWS)
-        tp[i] = (part[i] + dot(gk_n, w2[mine, cols])).astype(BF)
-        return 0
-
-    lax.fori_loop(0, 8, token_rest, 0)
-    swap = [links.send(tp.at[2 * i + other], tp_pair.at[i], sibling) for i in range(N_LOW)]
-    next(scatter)
-    for i in range(N_LOW):
-        swap[i].wait_recv()
-        tp[2 * i + core] = (tp[2 * i + core].astype(F32) + tp_pair[i].astype(F32)).astype(BF)
-    low_copies = [
-        links.send(tp.at[(low + d) % N_LOW * 2 + core], tp_low.at[d - 1], lows[d - 1]) for d in (1, 2, 3)
-    ]
-    for _ in scatter:
+    low_copies = []
+
+    def token_rest():
+        swap = []
+        for i in range(8):
+            block = i // 2 * 2 + (other if i % 2 == 0 else core)
+            cols = pl.ds(pl.multiple_of(block * ROWS, ROWS), ROWS)
+            tp[block] = (part[block] + dot(gk_n, w2[mine, cols])).astype(BF)
+            if i % 2 == 0:
+                swap.append(links.send(tp.at[block], tp_pair.at[i // 2], sibling))
+            if i % 2:
+                yield
+        for d in (1, 2, 3):
+            place = (low + d) % N_LOW
+            block = place * 2 + core
+            if d == 1:
+                for c in swap:
+                    c.wait_recv()
+            tp[block] = tp[block] + tp_pair[place]
+            low_copies.append(links.send(tp.at[block], tp_low.at[d - 1], lows[d - 1]))
+            yield
+        token_sum[...] = tp[head].astype(F32) + tp_pair[low].astype(F32)
+
+    side = token_rest()
+    for i, _ in enumerate(scatter_rows(links, g, landing, y, x, z, head)):
+        if i >= 3:
+            next(side, None)
+    for _ in side:
         pass
     own = g[y, x, z].astype(F32) + landing[5][0].astype(F32) + landing[5][1].astype(F32)
     pair_out[...] = own.astype(BF)
     last = links.send(pair_out, pair_in, sibling)
-    total = tp[head].astype(F32)
+    total = token_sum[...]
     for d in range(3):
         low_copies[d].wait_recv()
         total = total + tp_low[d].astype(F32)
     token_grad[...] = total.astype(BF)
+    put_token = put(1)
     last.wait_recv()
     weight_grad[0] = own + jnp.where(dp * 8 >= QC, pair_in[...].astype(F32), 0.0)
+    put_weight = put(2)
     links.finish()
+    put_attended.wait()
+    put_token.wait()
+    put_weight.wait()
 
 
 def body(tokens, weights, query_gain, key_gain, first_row, cotangent):
@@ -522,12 +604,22 @@
             jax.ShapeDtypeStruct((ROWS, D // 8), BF),
             jax.ShapeDtypeStruct((1, 8, D), F32),
         ),
-        in_specs=[WHOLE] * 7,
-        out_specs=[WHOLE] * 3,
+        in_specs=[pl.BlockSpec(memory_space=pl.ANY)] * 7,
+        out_specs=[pl.BlockSpec(memory_space=pl.ANY)] * 3,
         scratch_shapes=[
             pltpu.VMEM(BLOCKS, BF),
             pltpu.VMEM(BLOCKS, BF),
             *SCATTER_LANDING,
+            pltpu.VMEM((ROWS, D), BF),
+            pltpu.VMEM((1, HD), F32),
+            pltpu.VMEM((1, HD), F32),
+            pltpu.VMEM((1, HD), F32),
+            pltpu.VMEM((1, ROWS), jnp.int32),
+            pltpu.VMEM((ROWS, QC), BF),
+            pltpu.VMEM((ROWS, QC), BF),
+            pltpu.VMEM((ROWS, D // 8), BF),
+            pltpu.VMEM((1, 8, D), F32),
+            pltpu.SemaphoreType.DMA((10,)),
             pltpu.VMEM((8, D), BF),
             pltpu.VMEM((8, D), BF),
             pltpu.VMEM((D, ROWS), BF),
@@ -554,11 +646,12 @@
             pltpu.VMEM((8, ROWS, ROWS), BF),
             pltpu.VMEM((N_LOW, ROWS, ROWS), BF),
             pltpu.VMEM((N_LOW - 1, ROWS, ROWS), BF),
+            pltpu.VMEM((ROWS, ROWS), F32),
             pltpu.SemaphoreType.DMA((N_COPIES,)),
             pltpu.SemaphoreType.DMA((N_COPIES,)),
         ],
         compiler_params=pltpu.CompilerParams(
-            collective_id=1, has_side_effects=True, vmem_limit_bytes=50 << 20
+            collective_id=1, has_side_effects=True, vmem_limit_bytes=63 << 20
         ),
         cost_estimate=pl.CostEstimate(flops=4 * 10**9, bytes_accessed=4 << 20, transcendentals=10**6),
         name="masked_attention_layer",

time: 125 us -> 116 us (0.928); the launches traced: 124 us -> 116 us
  Pallas kernels: 117 us -> 112 us
  local copies, waits for them, and re-layouts: 5.6 us -> 3.2 us
    pallas_call x1, Pallas kernels: 117 us -> 112 us  [body(): pl.pallas_call(layer_kernel, out_shape=(jax.ShapeDtypeStruct((ROWS, QC),...]
    unnamed x17 -> x7, local copies, waits for them, and re-layouts: 5.6 us -> 3.2 us
where the time goes in v3:
time: 116 us
  Pallas kernels  112 us (97%)
  local copies, waits for them, and re-layouts  3.2 us (3%)
    pallas_call x1, Pallas kernels, body(): pl.pallas_call(layer_kernel, out_shape=(jax.ShapeDtypeStruct((ROWS, QC),...  112 us
    unnamed x7, local copies, waits for them, and re-layouts  3.2 us

profile of v3, /device:TPU:1, one launch (start us, length us, event | category | flops | bytes accessed | tf_op | source)
XLA Modules:
  0.0 116.1 jit_solution(13931189236230111078)
XLA Ops:
  0.6 112.2 %masked_attention_layer.1 = (bf16[256,512]{1,0:T(8,128)(2,1)}, bf16[256,256]{1,0:T(8,128)(2,1)}, f32[1,8,2048]{2,1,0:T(8,128)}) custom-call(bf16[256,2048]{1,0:T(8,128)(2,1)} %refs_0_.1, bf16[1,8,2048]{2,1,0:T(8,128)(2,1)} %refs_1_.1, f32[1,128]{1,0:T(1,128)} %bitcast.4, f32[1,128]{1,0:T(1,128)} %bitcast.5, f32[1,128]{1,0:T(1,128)} %constant.2.clone.refs_4_, ...), custom_call_target="tpu_custom_call" | custom-call | flops 4000000000 | bytes 4194304 | tf_op jit(solution)/shard_map/masked_attention_layer/pallas_call | solution.py:600
  112.9 0.0 copy-start
  112.9 1.7 %copy.13 = bf16[256,512]{1,0:T(8,128)(2,1)} copy(bf16[256,512]{1,0:T(8,128)(2,1)} %get-tuple-element.6) | data formatting | bytes 524288
  114.6 0.0 copy-done
  114.6 0.0 copy-start.1
  114.6 0.7 copy.14
  115.2 0.2 copy-done.1
  115.4 0.6 copy.15
Async XLA Ops:
  112.9 1.7 %copy-start = (bf16[256,256]{1,0:T(8,128)(2,1)S(1)}, bf16[256,256]{1,0:T(8,128)(2,1)}, u32[]{:S(2)}) copy-start(bf16[256,256]{1,0:T(8,128)(2,1)} %get-tuple-element.7) | copy-start | bytes 393220
  114.6 0.9 copy-start.1

commit v4 on v3

--- a/solution.py
+++ b/solution.py
@@ -27,7 +27,7 @@
 
 NY, NX, NZ = 8, 4, 3
 D = 2048
-CA = 1024
+CA = 768
 CB = D - CA
 CH = CB // 2
 MESH = pl.DeviceIdType.MESH
@@ -120,13 +120,16 @@
         r = w.at[y, x, k, :, A]
         s = [links.send(r, r, t) for t in (right, left, across)]
         yield
-        for step in range(4):
+        for step in range(3):
             arrived(s)
             s = []
-            for sign, t, half in ((-1, up, 0), (1, down, NX // 2)):
-                xs = pl.ds(0, NX) if step < 3 else pl.ds(half, NX // 2)
-                r = w.at[ry(y + sign * step), xs, k, :, A]
+            for sign, t, t2, half in ((-1, up, up2, 0), (1, down, down2, NX // 2)):
+                slab = ry(y + sign * step)
+                r = w.at[slab, :, k, :, A]
                 s.append(links.send(r, r, t))
+                if step == 2:
+                    r = w.at[slab, pl.ds(half, NX // 2), k, :, A]
+                    s.append(links.send(r, r, t2))
             yield
         arrived(s)
 
@@ -214,22 +217,26 @@
     def seq_a(d):
         k = rz(z + d)
         s = []
-        for step in range(4):
+        twice = []
+        for step in range(3):
             n = []
-            for i, (sign, t) in enumerate(((1, up), (-1, down))):
-                slab = ry(y + sign * (4 - step))
+            for i, (sign, t, t2) in enumerate(((1, up, up2), (-1, down, down2))):
+                slab = ry(y + sign * (3 - step))
                 half = pl.ds(i * (NX // 2), NX // 2)
                 if step:
                     s[i].wait_recv()
-                    xs = half if step == 1 else pl.ds(0, NX)
-                    add((slab, xs, k, rows, A), (lay, (k, i, step - 1, xs)))
-                xs = half if step == 0 else pl.ds(0, NX)
-                n.append(links.send(g.at[slab, xs, k, :, A], lay.at[k, i, step, xs], t))
+                    add((slab, pl.ds(0, NX), k, rows, A), (lay, (k, i, step - 1)))
+                if step == 1:
+                    twice[i].wait_recv()
+                    add((slab, half, k, rows, A), (lay, (k, i, 3, half)))
+                n.append(links.send(g.at[slab, :, k, :, A], lay.at[k, i, step], t))
+                if step == 0:
+                    twice.append(links.send(g.at[ry(y + 4), half, k, :, A], lay.at[k, i, 3, half], t2))
             s = n
             yield
         for c in s:
             c.wait_recv()
-        add((y, pl.ds(0, NX), k, rows, A), (lay, (k, 0, 3)), (lay, (k, 1, 3)))
+        add((y, pl.ds(0, NX), k, rows, A), (lay, (k, 0, 2)), (lay, (k, 1, 2)))
         s = [links.send(g.at[y, rx(x + e), k, :, A], lax_.at[k, e - 1], t)
              for e, t in ((1, right), (2, across), (3, left))]
         yield

time: 116 us -> 112 us (0.966)
  Pallas kernels: 112 us -> 108 us
    pallas_call x1, Pallas kernels: 112 us -> 108 us  [body(): pl.pallas_call(layer_kernel, out_shape=(jax.ShapeDtypeStruct((ROWS, QC),...]
where the time goes in v4:
time: 112 us
  Pallas kernels  108 us (96%)
  local copies, waits for them, and re-layouts  3.2 us (3%)
    pallas_call x1, Pallas kernels, body(): pl.pallas_call(layer_kernel, out_shape=(jax.ShapeDtypeStruct((ROWS, QC),...  108 us
    unnamed x7, local copies, waits for them, and re-layouts  3.2 us

profile of v4, /device:TPU:1, one launch (start us, length us, event | category | flops | bytes accessed | tf_op | source)
XLA Modules:
  0.0 112.1 jit_solution(1687997882837130167)
XLA Ops:
  0.6 108.2 %masked_attention_layer.1 = (bf16[256,512]{1,0:T(8,128)(2,1)}, bf16[256,256]{1,0:T(8,128)(2,1)}, f32[1,8,2048]{2,1,0:T(8,128)}) custom-call(bf16[256,2048]{1,0:T(8,128)(2,1)} %refs_0_.1, bf16[1,8,2048]{2,1,0:T(8,128)(2,1)} %refs_1_.1, f32[1,128]{1,0:T(1,128)} %bitcast.4, f32[1,128]{1,0:T(1,128)} %bitcast.5, f32[1,128]{1,0:T(1,128)} %constant.2.clone.refs_4_, ...), custom_call_target="tpu_custom_call" | custom-call | flops 4000000000 | bytes 4194304 | tf_op jit(solution)/shard_map/masked_attention_layer/pallas_call | solution.py:607
  108.9 0.0 copy-start
  108.9 1.7 %copy.13 = bf16[256,512]{1,0:T(8,128)(2,1)} copy(bf16[256,512]{1,0:T(8,128)(2,1)} %get-tuple-element.6) | data formatting | bytes 524288
  110.6 0.0 copy-done
  110.6 0.0 copy-start.1
  110.6 0.7 copy.14
  111.2 0.2 copy-done.1
  111.5 0.6 copy.15
Async XLA Ops:
  108.9 1.7 %copy-start = (bf16[256,256]{1,0:T(8,128)(2,1)S(1)}, bf16[256,256]{1,0:T(8,128)(2,1)}, u32[]{:S(2)}) copy-start(bf16[256,256]{1,0:T(8,128)(2,1)} %get-tuple-element.7) | copy-start | bytes 393220
  110.6 0.9 copy-start.1
